TPU v7x, 32 devices: a whole 2x2x4 slice. The times are simulated.
32 devices in a mesh: img: 2 (over x), row: 4 (over y, core), col: 4 (over z).
Axes of the slice: x: 2, y: 2, z: 4, core: 2. Of those that a mesh axis runs over, the one named last changes fastest.
Arguments:
- grid_elements: bfloat16 [256, 128, 768], P(('img', 'row'), 'col'), parts along dimension 0, may hold values from -6 to 6
- summary_vectors: bfloat16 [16, 8, 768], P(('img', 'row'), 'col'), parts along dimension 0, may hold values from -6 to 6
- triple_projection: bfloat16 [768, 2304], P(None, 'row'), may hold values from -0.375 to 0.375
- final_projection: bfloat16 [768, 768], P(None, 'row'), may hold values from -0.21875 to 0.21875
- genuine_flags: int32 [256, 128], P(('img', 'row'), 'col'), parts along dimension 0, may hold values 0 or 1
Outputs:
- element_result: bfloat16 [256, 128, 768], P(('img', 'row'), 'col'), parts along dimension 0
- summary_result: bfloat16 [16, 8, 768], P(('img', 'row'), 'col'), parts along dimension 0
There are 2 independent parts, one for each index of `img`. A program takes and returns all parts, laid end to end along the dimension named above; an argument that names none is the same for every part. Nothing has to cross between parts.
All inputs are finite; a program needn't handle non-finite values. No bound on the sum of `genuine_flags` on one device may be relied on, other than what follows from the above.
Results may differ from a plain program's by a relative error of at most 0.0096.
Values may be sent and summed in bfloat16 or wider, within the bound.
No kernel may reach another device: no remote copies, remote signals or barrier semaphores. Data moves between devices by JAX's collectives and lax.ppermute only.
A program may use at most 64 MiB of HBM per device.

v0:
```python
import functools

import jax
import jax.numpy as jnp
from jax import lax
from jax.experimental import pallas as pl
from jax.experimental.pallas import tpu as pltpu
from jax.sharding import PartitionSpec as P

HEAD_DIM = 64
PATCH_SIDE = 16
RADIUS = 4
TILE = 2 * RADIUS
LANES = 128
GROUP = 256
INVALID = 100.0
HIDDEN = -1e30
LOG2_E = 1.4426950408889634
EVEN_ROW, EVEN_COL, ROW, STARTS = 4, 5, 6, 7
VMEM_BYTES = 26 * 1024 * 1024


def nt(a, b):
    return lax.dot_general(a, b, (((1,), (1,)), ((), ())), preferred_element_type=jnp.float32)


def nn(a, b):
    return lax.dot_general(a, b, (((1,), (0,)), ((), ())), preferred_element_type=jnp.float32)


def layer_normalise(lines):
    center = lines - jnp.mean(lines, axis=-1, keepdims=True)
    spread = jnp.mean(center * center, axis=-1, keepdims=True)
    return center * lax.rsqrt(spread + 1e-05)


def pair_swapped(even_block, odd_block, axis):
    count = lax.axis_size(axis)
    got = []
    for first, block in ((0, even_block), (1, odd_block)):
        pairs = [(i, i + 1) for i in range(first, count - 1, 2)]
        got.append(lax.ppermute(block, axis, pairs + [(b, a) for a, b in pairs]))
    return got


def swapped(block, axis, bit):
    count = lax.axis_size(axis)
    return lax.ppermute(block, axis, [(i, i ^ bit) for i in range(count)])


def after(block, *others):
    return lax.optimization_barrier((block, *others))[0]


def bits_of(count):
    bits, bit = [], count // 2
    while bit:
        bits.append(bit)
        bit //= 2
    return bits


def marked_lanes(lines, hidden):
    first = jnp.where(hidden, INVALID, lines[:, :, :LANES])
    return jnp.concatenate([first, lines[:, :, LANES:]], axis=2)


def edge_kernel(place_ref, flags_hbm, x_hbm, mark_ref, even_ref, odd_ref, x_ref, *scratch):
    flags_ref, spread, sems = scratch
    rows, cols = flags_ref.shape
    flags_copy = pltpu.make_async_copy(flags_hbm, flags_ref, sems.at[0])
    x_copy = pltpu.make_async_copy(x_hbm, x_ref, sems.at[1])
    flags_copy.start()
    x_copy.start()
    flags_copy.wait()
    row_at = lax.broadcasted_iota(jnp.int32, (cols, cols), 0)
    diagonal = row_at == lax.broadcasted_iota(jnp.int32, (cols, cols), 1)
    for r in range(rows):
        hidden = jnp.where(flags_ref[r : r + 1, :] > 0, 0.0, INVALID)
        spread[r * cols : (r + 1) * cols, :] = jnp.where(diagonal, hidden, 0.0).astype(jnp.bfloat16)
    marks = nn(spread[...], jnp.ones((cols, LANES), jnp.bfloat16)).reshape(rows, cols, LANES)
    mark_ref[...] = marks.astype(jnp.bfloat16)
    x_copy.wait()
    first, last = [
        marked_lanes(x_ref[at].astype(jnp.float32), marks[at] > INVALID / 2)
        for at in (slice(0, RADIUS), slice(rows - RADIUS, rows))
    ]
    even = place_ref[EVEN_ROW] > 0
    even_ref[...] = jnp.where(even, last, first).astype(jnp.bfloat16)
    odd_ref[...] = jnp.where(even, first, last).astype(jnp.bfloat16)


def piece_kernel(place_ref, triple_hbm, mine_ref, last_ref, sems):
    start = pl.multiple_of(place_ref[STARTS], 16)
    last = triple_hbm.shape[0] - last_ref.shape[0]
    copies = [
        pltpu.make_async_copy(triple_hbm.at[pl.ds(start, mine_ref.shape[0]), :], mine_ref, sems.at[0]),
        pltpu.make_async_copy(triple_hbm.at[last:, :], last_ref, sems.at[1]),
    ]
    for copy in copies:
        copy.start()
    for copy in copies:
        copy.wait()


def strip_kernel(place_ref, x_ref, mark_ref, even_rows_ref, odd_rows_ref, carriers_ref, even_ref, odd_ref, carriers_s):
    per_row = carriers_ref.shape[1]
    carriers_s[...] = jnp.zeros_like(carriers_s)
    for i in range(carriers_ref.shape[0]):
        carriers_s[i * per_row : (i + 1) * per_row, :] = carriers_ref[i].astype(jnp.float32)
    for i in range(carriers_s.shape[0] // TILE):
        even_ref[odd_ref.shape[0] + i] = carriers_s[i * TILE : (i + 1) * TILE, :].astype(jnp.bfloat16)
    rows, cols, channels = x_ref.shape
    middle = rows // 2
    low = lax.broadcasted_iota(jnp.int32, (1, TILE, 1), 1) < RADIUS
    even_row, even_col = place_ref[EVEN_ROW] > 0, place_ref[EVEN_COL] > 0
    for lane in range(0, channels, LANES):
        lanes = slice(lane, lane + LANES)
        strips = []
        for columns, last in ((slice(0, TILE), False), (slice(cols - TILE, cols), True)):

            def own(part):
                lines = x_ref[part, columns, lanes].astype(jnp.float32)
                if lane == 0:
                    lines = jnp.where(mark_ref[part, columns, :].astype(jnp.float32) > INVALID / 2, INVALID, lines)
                return lines

            even_rows = even_rows_ref[:, columns, lanes].astype(jnp.float32)
            odd_rows = odd_rows_ref[:, columns, lanes].astype(jnp.float32)
            top, bottom = jnp.where(even_row, odd_rows, even_rows), jnp.where(even_row, even_rows, odd_rows)
            upper = jnp.concatenate([top, own(slice(0, middle))], axis=0)
            lower = jnp.concatenate([own(slice(middle, rows)), bottom], axis=0)
            if last:
                upper = jnp.roll(upper, RADIUS, axis=1)
            else:
                lower = jnp.roll(lower, RADIUS, axis=1)
            strips.append(jnp.where(low, upper, lower))
        first, last = strips
        even_ref[: odd_ref.shape[0], :, lanes] = jnp.where(even_col, last, first).astype(jnp.bfloat16)
        odd_ref[:, :, lanes] = jnp.where(even_col, first, last).astype(jnp.bfloat16)


def carrier_pair_kernel(own_ref, got_hbm, out_ref, got_s, pair_s, sem):
    per_row, here = own_ref.shape[1], own_ref.shape[0] * own_ref.shape[1]
    tiles = got_s.shape[0]
    copy = pltpu.make_async_copy(got_hbm.at[got_hbm.shape[0] - tiles :], got_s, sem)
    copy.start()
    for i in range(own_ref.shape[0]):
        pair_s[i * per_row : (i + 1) * per_row, :] = own_ref[i].astype(jnp.float32)
    copy.wait()
    pair_s[here:, :] = got_s[...].astype(jnp.float32).reshape(tiles * TILE, -1)[:here]
    out_ref[...] = pair_s[...].astype(jnp.bfloat16)


def pack_kernel(final_hbm, *refs):
    parts, (out_ref, sem) = refs[:-2], refs[-2:]
    rows = final_hbm.shape[0]
    copy = pltpu.make_async_copy(final_hbm, out_ref.at[0:rows, :], sem)
    copy.start()
    carriers = jnp.concatenate([part[...].astype(jnp.float32) for part in parts], axis=0)
    out_ref[rows:, :] = carriers.astype(jnp.bfloat16)
    copy.wait()


def own_kernel(x_ref, xq_ref):
    rows, cols, _ = x_ref.shape
    step = 4

    def own(i, _):
        at = pl.multiple_of(i * step, step)
        y = layer_normalise(x_ref[pl.ds(at, step)].astype(jnp.float32))
        for c in range(cols // TILE):
            piece = y[:, c * TILE : (c + 1) * TILE, :].reshape(step * TILE, -1)
            to = pl.multiple_of(c * rows * TILE + at * TILE, step * TILE)
            xq_ref[pl.ds(to, step * TILE), :] = piece.astype(jnp.bfloat16)
        return 0

    lax.fori_loop(0, rows // step, own, 0)


def halo_kernel(place_ref, xq_ref, mark_ref, even_rows_ref, odd_rows_ref, even_cols_ref, odd_cols_ref, xkv_ref, hide_ref, *scratch):
    rows, cols, _ = mark_ref.shape
    wide_rows, wide_cols = rows + 2 * RADIUS, cols + 2 * RADIUS
    half = wide_rows // 2
    step = 2
    top_s, bottom_s, left_s, right_s, top_ref, bottom_ref, left_ref, right_ref, flag_s = scratch
    for even, odd, low, high, low_flags, high_flags, parity, size in (
        (even_rows_ref, odd_rows_ref, top_s, bottom_s, top_ref, bottom_ref, EVEN_ROW, 2),
        (even_cols_ref, odd_cols_ref, left_s, right_s, left_ref, right_ref, EVEN_COL, 5),
    ):
        flip = place_ref[parity] > 0
        for i in range(0, odd.shape[0], size):
            a, b = even[i : i + size].astype(jnp.float32), odd[i : i + size].astype(jnp.float32)
            for lines, out, flags in ((jnp.where(flip, b, a), low, low_flags), (jnp.where(flip, a, b), high, high_flags)):
                out[i : i + size] = layer_normalise(lines)
                flags[i : i + size] = lines[:, :, :LANES]

    def lines_of(ref):
        return ref.astype(jnp.float32)

    def merge(at, blocks, left, right, to_ref):
        low = lax.broadcasted_iota(jnp.int32, (1, TILE, 1), 1) < RADIUS
        before = left
        for c in range(len(blocks) + 1):
            after = jnp.roll(blocks[c], RADIUS, axis=1) if c < len(blocks) else right
            to = c * wide_rows * TILE + at * TILE
            to = pl.multiple_of(to, step * TILE) if not isinstance(to, int) else to
            lines = jnp.where(low, before, after).reshape(step * TILE, -1)
            to_ref[pl.ds(to, step * TILE), :] = lines.astype(jnp.bfloat16)
            before = after

    def sides(at, upper, left_ref, right_ref, lanes):
        if upper:
            at = at - half
            left, right = jnp.roll(lines_of(left_ref[pl.ds(at, step), :, lanes]), RADIUS, axis=1), lines_of(
                right_ref[pl.ds(at, step), :, lanes]
            )
        else:
            left, right = lines_of(left_ref[pl.ds(at, step), :, lanes]), jnp.roll(
                lines_of(right_ref[pl.ds(at, step), :, lanes]), RADIUS, axis=1
            )
        return left, right

    every, few = slice(None), slice(0, LANES)

    def hide_if(border, lines):
        return jnp.where(place_ref[border] > 0, INVALID, lines)

    def mark_sides(at, upper):
        left, right = sides(at, upper, left_ref, right_ref, few)
        return hide_if(2, left), hide_if(3, right)

    def band(at, ref, ref_s, first, upper):
        cut = [slice(c * TILE, (c + 1) * TILE) for c in range(cols // TILE)]
        merge(at, [ref_s[first : first + step, k, :] for k in cut], *sides(at, upper, left_s, right_s, every), xkv_ref)
        marks = hide_if(int(upper), ref[first : first + step])
        beside = [hide_if(int(upper), side) for side in mark_sides(at, upper)]
        merge(at, [marks[:, k, :] for k in cut], *beside, flag_s)

    for i in range(0, RADIUS, step):
        band(i, top_ref, top_s, i, False)
        band(RADIUS + rows + i, bottom_ref, bottom_s, i, True)

    def middle(i, upper):
        at = pl.multiple_of(i * step, step)
        own = at - RADIUS
        blocks = []
        for c in range(cols // TILE):
            first = pl.multiple_of(c * rows * TILE + own * TILE, step * TILE)
            blocks.append(xq_ref[pl.ds(first, step * TILE), :].astype(jnp.float32).reshape(step, TILE, -1))
        merge(at, blocks, *sides(at, upper, left_s, right_s, every), xkv_ref)
        marks = mark_ref[pl.ds(own, step)].astype(jnp.float32)
        marks = [marks[:, c * TILE : (c + 1) * TILE, :] for c in range(cols // TILE)]
        merge(at, marks, *mark_sides(at, upper), flag_s)
        return 0

    lax.fori_loop(RADIUS // step, half // step, lambda i, _: middle(i, False), 0)
    lax.fori_loop(half // step, (RADIUS + rows) // step, lambda i, _: middle(i, True), 0)

    first_lane = (lax.broadcasted_iota(jnp.int32, (8, LANES), 1) == 0).astype(jnp.bfloat16)
    spans = []
    for c in range(wide_cols // TILE):
        lines = flag_s[c * wide_rows * TILE : (c + 1) * wide_rows * TILE, :]
        spans.append(jnp.where(nt(first_lane, lines) > INVALID / 2, HIDDEN, 0.0))
    tall = rows // TILE
    for c in range(cols // TILE):
        for r in range(tall):
            at = slice(r * TILE * TILE, r * TILE * TILE + 2 * TILE * TILE)
            hide_ref[c * tall + r] = jnp.concatenate([spans[c][:, at], spans[c + 1][:, at]], axis=1)


def project_kernel(whole, pieces, triple_rows, place_ref, *refs):
    sources, refs = refs[: len(whole) + len(pieces)], refs[len(whole) + len(pieces) :]
    xq_ref, xkv_ref, q_s, k_s, v_s, wt, sems = refs
    channels = wt.shape[1]
    groups = channels // GROUP
    factor = HEAD_DIM ** (-0.5) * LOG2_E
    me = place_ref[ROW]
    copies = []
    for j, source in enumerate(sources):
        if j < len(whole):
            to = (me ^ whole[j]) * triple_rows
        else:
            off, start = pieces[j - len(whole)]
            to = (me ^ off) * triple_rows + place_ref[STARTS + start]
        to = pl.multiple_of(to, 16)
        copy = pltpu.make_async_copy(source, wt.at[pl.ds(to, source.shape[0]), :], sems.at[j])
        copy.start()
        copies.append(copy)
    for copy in copies:
        copy.wait()

    q_rows, kv_rows = xq_ref.shape[0], xkv_ref.shape[0]
    q_chunk, kv_chunk = q_rows // 2, kv_rows // 4

    def project_q(n, _):
        w = wt[pl.ds(pl.multiple_of(n * GROUP, GROUP), GROUP), :]
        for m in range(0, q_rows, q_chunk):
            q_s[n, m : m + q_chunk, :] = (nt(xq_ref[m : m + q_chunk, :], w) * factor).astype(jnp.bfloat16)
        return 0

    def project_k(n, _):
        w = wt[pl.ds(pl.multiple_of(channels + n * GROUP, GROUP), GROUP), :]
        for m in range(0, kv_rows, kv_chunk):
            k_s[n, m : m + kv_chunk, :] = nt(xkv_ref[m : m + kv_chunk, :], w).astype(jnp.bfloat16)
        return 0

    def project_v(n, _):
        w = wt[pl.ds(pl.multiple_of(2 * channels + n * GROUP, GROUP), GROUP), :]
        for m in range(0, kv_rows, kv_chunk):
            v_s[n, m : m + kv_chunk, :] = nt(xkv_ref[m : m + kv_chunk, :], w).astype(jnp.bfloat16)
        return 0

    lax.fori_loop(0, groups, project_q, 0)
    lax.fori_loop(0, groups, project_k, 0)
    lax.fori_loop(0, groups, project_v, 0)


def carrier_kernel(offsets, place_ref, wt, *refs):
    shards = len(offsets)
    finals, refs = refs[:shards], refs[shards:]
    summary_ref, wo, kce, vc_s, carriers_s, sems = refs
    per_row = summary_ref.shape[1]
    channels = wt.shape[1]
    groups = channels // GROUP
    heads = channels // HEAD_DIM
    factor = HEAD_DIM ** (-0.5)
    carriers_here = vc_s.shape[0]
    final_rows = wo.shape[0] // shards
    copies = []
    for j, off in enumerate(offsets):
        to = pl.multiple_of((place_ref[ROW] ^ off) * final_rows, 16)
        copy = pltpu.make_async_copy(finals[j].at[0:final_rows, :], wo.at[pl.ds(to, final_rows), :], sems.at[j])
        copy.start()
        copies.append(copy)
    coming = []
    sent = carriers_s.shape[0] // shards
    for j in range(shards):
        source = finals[j].at[final_rows : final_rows + sent, :]
        copy = pltpu.make_async_copy(source, carriers_s.at[j * sent : (j + 1) * sent, :], sems.at[shards + j])
        copy.start()
        coming.append(copy)
    for copy in coming:
        copy.wait()
    carriers = carriers_s[...].astype(jnp.float32)
    own = carriers[:carriers_here]
    carriers = layer_normalise(carriers).astype(jnp.bfloat16)
    own_norm = layer_normalise(own).astype(jnp.bfloat16)
    qc = (nt(own_norm, wt[:channels, :]) * factor).astype(jnp.bfloat16).astype(jnp.float32)
    kc = nt(carriers, wt[channels : 2 * channels, :]).astype(jnp.bfloat16)
    vc = nt(carriers, wt[2 * channels :, :]).astype(jnp.bfloat16)
    head_of = lax.broadcasted_iota(jnp.int32, (1, channels), 1) // HEAD_DIM
    stacked = jnp.concatenate([jnp.where(head_of == h, qc, 0.0) for h in range(heads)], axis=0)
    e = jnp.exp(nt(stacked.astype(jnp.bfloat16), kc))
    weights = (e / jnp.sum(e, axis=-1, keepdims=True)).astype(jnp.bfloat16)
    o = nn(weights, vc)
    mix = jnp.zeros((carriers_here, channels), jnp.float32)
    for h in range(heads):
        mix = jnp.where(head_of == h, o[h * carriers_here : (h + 1) * carriers_here, :], mix)
    for copy in copies:
        copy.wait()
    renewed = own + nt(mix.astype(jnp.bfloat16), wo[...])
    for i in range(summary_ref.shape[0]):
        summary_ref[i] = renewed[i * per_row : (i + 1) * per_row, :].astype(jnp.bfloat16)
    fresh = nt(layer_normalise(renewed).astype(jnp.bfloat16), wt[channels:, :]).astype(jnp.bfloat16).astype(jnp.float32)
    vc_s[...] = fresh[:, channels:]
    same = (
        lax.broadcasted_iota(jnp.int32, (GROUP, GROUP), 0) // HEAD_DIM
        == lax.broadcasted_iota(jnp.int32, (GROUP, GROUP), 1) // HEAD_DIM
    )
    windows = kce.shape[0] // groups
    for w in range(windows):
        for g in range(groups):
            kce[w * groups + g] = jnp.where(same, fresh[w : w + 1, g * GROUP : (g + 1) * GROUP], 0.0).astype(jnp.bfloat16)


def attend_kernel(tall, broad, q_s, k_s, v_s, hide_ref, kce, vc_s, mix_s, pc_s, even_s, odd_s):
    groups, tiles = q_s.shape[0], hide_ref.shape[0]
    heads_in = GROUP // HEAD_DIM
    queries, span = TILE * TILE, 2 * TILE * TILE
    side = PATCH_SIDE // TILE
    wide = (tall + 1) * queries
    qi = lax.broadcasted_iota(jnp.int32, (queries, 2 * span), 0)
    ki = lax.broadcasted_iota(jnp.int32, (queries, 2 * span), 1)
    row_step = (ki % span) // TILE - qi // TILE
    col_step = (ki // span) * TILE + ki % TILE - qi % TILE
    seen = (row_step >= 0) & (row_step <= 2 * RADIUS) & (col_step >= 0) & (col_step <= 2 * RADIUS)
    band = jnp.where(seen, 0.0, HIDDEN)
    group_head = lax.broadcasted_iota(jnp.int32, (1, GROUP), 1) // HEAD_DIM
    only = [jnp.where(group_head == h, 1.0, 0.0).astype(jnp.bfloat16) for h in range(heads_in)]
    in_pair = LANES // HEAD_DIM
    pair_head = lax.broadcasted_iota(jnp.int32, (1, LANES), 1) // HEAD_DIM

    for c in range(broad):
        for w in range(tall // side):
            at = slice((c * tall + w * side) * queries, (c * tall + (w + 1) * side) * queries)
            window = w * (broad // side) + c // side
            for g in range(groups):
                pc_s[at, g * GROUP : (g + 1) * GROUP] = jnp.exp2(nt(q_s[g, at, :], kce[window * groups + g]))

    def keys_at(t):
        k0 = pl.multiple_of(t // tall * wide + t % tall * queries, queries)
        return k0, pl.multiple_of(k0 + wide, queries)

    def scores(t, ref):
        q_at = pl.multiple_of(t * queries, queries)
        k0, k1 = keys_at(t)
        for g in range(groups):
            q = q_s[g, pl.ds(q_at, queries), :]
            qq = jnp.concatenate([q * mask for mask in only], axis=0)
            k = jnp.concatenate([k_s[g, pl.ds(k0, span), :], k_s[g, pl.ds(k1, span), :]], axis=0)
            ref[g] = nt(qq, k)

    def finish(t, ref):
        q_at = pl.multiple_of(t * queries, queries)
        k0, k1 = keys_at(t)
        window = t % tall // side * (broad // side) + t // tall // side
        bias = band + hide_ref[t][0:1, :]
        for g in range(groups):
            p = jnp.exp2(ref[g].reshape(heads_in, queries, 2 * span) + bias[None])
            total = jnp.sum(p, axis=-1, keepdims=True)
            v = jnp.concatenate([v_s[g, pl.ds(k0, span), :], v_s[g, pl.ds(k1, span), :]], axis=0)
            o = nn(p.reshape(heads_in * queries, 2 * span).astype(jnp.bfloat16), v).reshape(heads_in, queries, GROUP)
            v_new = vc_s[pl.ds(window, 1), g * GROUP : (g + 1) * GROUP]
            for j in range(GROUP // LANES):
                lanes = slice(j * LANES, (j + 1) * LANES)
                at = slice(g * GROUP + j * LANES, g * GROUP + (j + 1) * LANES)
                kept, kept_total = o[j * in_pair, :, lanes], total[j * in_pair]
                for h in range(1, in_pair):
                    kept = jnp.where(pair_head == h, o[j * in_pair + h, :, lanes], kept)
                    kept_total = jnp.where(pair_head == h, total[j * in_pair + h], kept_total)
                new = pc_s[pl.ds(q_at, queries), at]
                mixed = (kept + new * v_new[:, lanes]) / (kept_total + new)
                mix_s[pl.ds(q_at, queries), at] = mixed.astype(jnp.bfloat16)

    scores(0, even_s)

    def two(i, _):
        t = 2 * i
        scores(t + 1, odd_s)
        finish(t, even_s)
        scores(jnp.minimum(t + 2, tiles - 1), even_s)
        finish(t + 1, odd_s)
        return 0

    lax.fori_loop(0, tiles // 2, two, 0)


def out_kernel(x_ref, mix_s, wo, out_hbm, out_ref, out_sems):
    rows, cols, channels = x_ref.shape
    going = []
    for pair in range(cols // (2 * TILE)):
        both = slice(2 * pair * TILE, 2 * (pair + 1) * TILE)
        for g in range(channels // GROUP):
            at = slice(g * GROUP, (g + 1) * GROUP)
            w = wo[at, :]
            y = nt(mix_s[2 * pair * rows * TILE : 2 * (pair + 1) * rows * TILE, :], w).reshape(2, rows, TILE, GROUP)
            y = jnp.concatenate([y[0], y[1]], axis=1) + x_ref[:, both, at].astype(jnp.float32)
            out_ref[pair, :, :, at] = y.astype(jnp.bfloat16)
        copy = pltpu.make_async_copy(out_ref.at[pair], out_hbm.at[:, both, :], out_sems.at[pair])
        copy.start()
        going.append(copy)
    for copy in going:
        copy.wait()


def local(grid_elements, summary_vectors, triple_projection, final_projection, genuine_flags):
    rows, cols, channels = grid_elements.shape
    wide_rows, wide_cols = rows + 2 * RADIUS, cols + 2 * RADIUS

    triple_t, final_t = triple_projection.T, final_projection.T
    vmem = pl.BlockSpec(memory_space=pltpu.VMEM)
    anywhere = pl.BlockSpec(memory_space=pl.ANY)
    scalars = pl.BlockSpec(memory_space=pltpu.SMEM)
    hbm = pl.BlockSpec(memory_space=pltpu.HBM)
    small = pltpu.CompilerParams(vmem_limit_bytes=8 * 1024 * 1024)
    row_strip = jax.ShapeDtypeStruct((RADIUS, cols, channels), jnp.bfloat16)
    col_strip = jax.ShapeDtypeStruct((wide_rows // 2, 2 * RADIUS, channels), jnp.bfloat16)

    row, col, img = lax.axis_size("row"), lax.axis_size("col"), lax.axis_size("img")
    row_at, col_at, img_at = lax.axis_index("row"), lax.axis_index("col"), lax.axis_index("img")
    row_bits = bits_of(row)
    far, rest = row_bits[0], row_bits[1:]
    relays = img if triple_t.shape[0] % (16 * (img + 1)) == 0 else 0
    piece_rows = triple_t.shape[0] // (relays + 1)
    starts = [(img_at - k) % img for k in range(relays)] + [jnp.int32(relays)]
    place = [row_at == 0, row_at == row - 1, col_at == 0, col_at == col - 1, row_at % 2 == 0, col_at % 2 == 0, row_at]
    place = jnp.stack([jnp.asarray(p).astype(jnp.int32) for p in place + [start * piece_rows for start in starts]])

    mark, even_rows, odd_rows, x = pl.pallas_call(
        edge_kernel,
        out_shape=(
            pltpu.VMEM((rows, cols, LANES), jnp.bfloat16),
            pltpu.VMEM(row_strip.shape, jnp.bfloat16),
            pltpu.VMEM(row_strip.shape, jnp.bfloat16),
            pltpu.VMEM(grid_elements.shape, jnp.bfloat16),
        ),
        in_specs=[scalars, hbm, hbm],
        out_specs=(vmem,) * 4,
        scratch_shapes=[
            pltpu.VMEM((rows, cols), jnp.int32),
            pltpu.VMEM((rows * cols, cols), jnp.bfloat16),
            pltpu.SemaphoreType.DMA((2,)),
        ],
        compiler_params=small,
        cost_estimate=pl.CostEstimate(flops=1_000_000, bytes_accessed=1_000_000, transcendentals=0),
        name="edge_rows",
    )(place, *(pltpu.with_memory_space_constraint(a, pltpu.HBM) for a in (genuine_flags, grid_elements)))
    mine, last = pl.pallas_call(
        piece_kernel,
        out_shape=(
            pltpu.VMEM((piece_rows, channels), jnp.bfloat16),
            pltpu.VMEM((triple_t.shape[0] - relays * piece_rows, channels), jnp.bfloat16),
        ),
        in_specs=[scalars, hbm],
        out_specs=(vmem, vmem),
        scratch_shapes=[pltpu.SemaphoreType.DMA((2,))],
        compiler_params=small,
        cost_estimate=pl.CostEstimate(flops=1_000_000, bytes_accessed=1_000_000, transcendentals=0),
        name="pieces",
    )(place, pltpu.with_memory_space_constraint(after(triple_t, even_rows), pltpu.HBM))
    xq = pl.pallas_call(
        own_kernel,
        out_shape=pltpu.VMEM((rows * cols, channels), jnp.bfloat16),
        in_specs=[vmem],
        out_specs=vmem,
        compiler_params=small,
        cost_estimate=pl.CostEstimate(flops=1_000_000, bytes_accessed=1_000_000, transcendentals=0),
        name="own_norm",
    )(x)
    even_rows, odd_rows = pair_swapped(even_rows, odd_rows, "row")

    far_pieces = []
    if relays:
        first = swapped(mine, "row", far)
    far_last = swapped(after(last, even_rows, odd_rows), "row", far)

    own_rows = summary_vectors.shape[0] * summary_vectors.shape[1]
    carrier_tiles = -(-own_rows // TILE)
    even_cols, odd_cols = pl.pallas_call(
        strip_kernel,
        out_shape=(
            pltpu.VMEM((col_strip.shape[0] + carrier_tiles, *col_strip.shape[1:]), jnp.bfloat16),
            pltpu.VMEM(col_strip.shape, jnp.bfloat16),
        ),
        in_specs=[scalars] + [vmem] * 5,
        out_specs=(vmem,) * 2,
        scratch_shapes=[pltpu.VMEM((carrier_tiles * TILE, channels), jnp.float32)],
        compiler_params=small,
        cost_estimate=pl.CostEstimate(flops=1_000_000, bytes_accessed=2_000_000, transcendentals=0),
        name="edge_columns",
    )(place, x, after(mark, xq), even_rows, odd_rows, summary_vectors)
    even_cols, odd_cols = pair_swapped(even_cols, odd_cols, "col")
    carriers = pl.pallas_call(
        carrier_pair_kernel,
        out_shape=pltpu.VMEM((2 * own_rows, channels), jnp.bfloat16),
        in_specs=[vmem, anywhere],
        out_specs=vmem,
        scratch_shapes=[
            pltpu.VMEM((carrier_tiles, TILE, channels), jnp.bfloat16),
            pltpu.VMEM((2 * own_rows, channels), jnp.float32),
            pltpu.SemaphoreType.DMA,
        ],
        compiler_params=small,
        cost_estimate=pl.CostEstimate(flops=1_000, bytes_accessed=1_000, transcendentals=0),
        name="carrier_pair",
    )(summary_vectors, even_cols)
    parts = [carriers]
    for bit in bits_of(col)[:-1]:
        carriers = carriers if len(parts) == 1 else jnp.concatenate(parts, axis=0)
        got = swapped(carriers, "col", bit)
        parts.append(got)
    if relays:
        first = after(first, even_cols, odd_cols)
        others = [lax.ppermute(first, "img", [(i, (i + k) % img) for i in range(img)]) for k in range(1, relays)]
        far_pieces = [first] + others
    far_pieces.append(far_last)

    final_pack = pl.pallas_call(
        pack_kernel,
        out_shape=pltpu.VMEM((final_t.shape[0] + col * own_rows, channels), jnp.bfloat16),
        in_specs=[hbm] + [vmem] * len(parts),
        out_specs=vmem,
        scratch_shapes=[pltpu.SemaphoreType.DMA],
        compiler_params=small,
        cost_estimate=pl.CostEstimate(flops=1_000, bytes_accessed=1_000, transcendentals=0),
        name="final_pack",
    )(pltpu.with_memory_space_constraint(final_t, pltpu.HBM), *parts)
    finals, triples, offsets = [final_pack], [triple_t], [0]
    for bit in rest:
        finals = finals + [swapped(p, "row", bit) for p in finals]
        triples = triples + [swapped(p, "row", bit) for p in triples]
        offsets = offsets + [o ^ bit for o in offsets]
    tiles = (rows // TILE) * (cols // TILE)
    keys = 4 * TILE * TILE
    xkv, hide = pl.pallas_call(
        halo_kernel,
        out_shape=(
            pltpu.VMEM((wide_rows * wide_cols, channels), jnp.bfloat16),
            pltpu.VMEM((tiles, 8, keys), jnp.float32),
        ),
        in_specs=[scalars] + [vmem] * 6,
        out_specs=(vmem,) * 2,
        scratch_shapes=[
            *[pltpu.VMEM(shape.shape, jnp.float32) for shape in (row_strip, row_strip, col_strip, col_strip)],
            *[pltpu.VMEM((*shape.shape[:2], LANES), jnp.float32) for shape in (row_strip, row_strip, col_strip, col_strip)],
            pltpu.VMEM((wide_rows * wide_cols, LANES), jnp.bfloat16),
        ],
        compiler_params=pltpu.CompilerParams(vmem_limit_bytes=12 * 1024 * 1024),
        cost_estimate=pl.CostEstimate(flops=10_000_000, bytes_accessed=6_000_000, transcendentals=1000),
        name="halo_norm",
    )(place, after(xq, got), mark, even_rows, odd_rows, even_cols, odd_cols)

    far_final = swapped(final_pack, "row", far)

    far_offsets = [far]
    far_pieces = [[after(piece, xkv)] for piece in far_pieces]
    for bit in rest:
        far_pieces = [same + [swapped(p, "row", bit) for p in same] for same in far_pieces]
        far_offsets = far_offsets + [o ^ bit for o in far_offsets]

    groups = channels // GROUP
    numbered = [(off, number) for number in range(len(far_pieces)) for off in far_offsets]
    sources = triples + [piece for same in far_pieces for piece in same]
    q, k, v, wt = pl.pallas_call(
        functools.partial(project_kernel, offsets, numbered, triple_t.shape[0]),
        out_shape=(
            jax.ShapeDtypeStruct((groups, rows * cols, GROUP), jnp.bfloat16),
            jax.ShapeDtypeStruct((groups, wide_rows * wide_cols, GROUP), jnp.bfloat16),
            jax.ShapeDtypeStruct((groups, wide_rows * wide_cols, GROUP), jnp.bfloat16),
            jax.ShapeDtypeStruct((3 * channels, channels), jnp.bfloat16),
        ),
        in_specs=[scalars] + [anywhere] * len(sources) + [vmem] * 2,
        out_specs=(vmem,) * 4,
        scratch_shapes=[pltpu.SemaphoreType.DMA((len(sources),))],
        compiler_params=pltpu.CompilerParams(vmem_limit_bytes=VMEM_BYTES),
        cost_estimate=pl.CostEstimate(flops=5_000_000_000, bytes_accessed=14_000_000, transcendentals=0),
        name="project",
    )(place, *sources, xq, xkv)

    far_finals = [after(far_final, q)]
    for bit in rest:
        far_finals = far_finals + [swapped(p, "row", bit) for p in far_finals]
    finals, offsets = finals + far_finals, offsets + far_offsets
    carriers_here = carrier_tiles * TILE
    summary_result, wo, kce, vc = pl.pallas_call(
        functools.partial(carrier_kernel, offsets),
        out_shape=(
            jax.ShapeDtypeStruct(summary_vectors.shape, jnp.bfloat16),
            jax.ShapeDtypeStruct((channels, channels), jnp.bfloat16),
            jax.ShapeDtypeStruct((own_rows * groups, GROUP, GROUP), jnp.bfloat16),
            jax.ShapeDtypeStruct((carriers_here, channels), jnp.float32),
        ),
        in_specs=[scalars, vmem] + [anywhere] * len(finals),
        out_specs=(vmem,) * 4,
        scratch_shapes=[
            pltpu.VMEM((row * col * own_rows, channels), jnp.bfloat16),
            pltpu.SemaphoreType.DMA((2 * len(finals),)),
        ],
        compiler_params=pltpu.CompilerParams(vmem_limit_bytes=VMEM_BYTES),
        cost_estimate=pl.CostEstimate(flops=500_000_000, bytes_accessed=5_000_000, transcendentals=10_000),
        name="carriers",
    )(place, wt, *finals)

    scores = (groups, GROUP // HEAD_DIM * TILE * TILE, keys)
    mix = pl.pallas_call(
        functools.partial(attend_kernel, rows // TILE, cols // TILE),
        out_shape=jax.ShapeDtypeStruct((rows * cols, channels), jnp.bfloat16),
        in_specs=[vmem] * 6,
        out_specs=vmem,
        scratch_shapes=[
            pltpu.VMEM((rows * cols, channels), jnp.float32),
            pltpu.VMEM(scores, jnp.float32),
            pltpu.VMEM(scores, jnp.float32),
        ],
        compiler_params=pltpu.CompilerParams(vmem_limit_bytes=VMEM_BYTES),
        cost_estimate=pl.CostEstimate(flops=4_000_000_000, bytes_accessed=12_000_000, transcendentals=4_000_000),
        name="attend",
    )(q, k, v, hide, kce, vc)

    out = pl.pallas_call(
        out_kernel,
        out_shape=jax.ShapeDtypeStruct(grid_elements.shape, jnp.bfloat16),
        in_specs=[vmem] * 3,
        out_specs=anywhere,
        scratch_shapes=[
            pltpu.VMEM((cols // (2 * TILE), rows, 2 * TILE, channels), jnp.bfloat16),
            pltpu.SemaphoreType.DMA((cols // (2 * TILE),)),
        ],
        compiler_params=pltpu.CompilerParams(vmem_limit_bytes=VMEM_BYTES),
        cost_estimate=pl.CostEstimate(flops=1_200_000_000, bytes_accessed=6_000_000, transcendentals=0),
        name="out",
    )(x, mix, wo)
    return (out, summary_result)


def solution(mesh):
    placed = (
        P(("img", "row"), "col", None),
        P(("img", "row"), "col", None),
        P(None, "row"),
        P(None, "row"),
        P(("img", "row"), "col"),
    )
    return jax.shard_map(
        local,
        mesh=mesh,
        in_specs=placed,
        out_specs=(P(("img", "row"), "col", None), P(("img", "row"), "col", None)),
        check_vma=False,
    )
```

profile of v0, /device:TPU:0, one launch (start us, length us, event | category | flops | bytes accessed | tf_op | source)
XLA Modules:
  0.0 58.7 jit_solution(8367576591953681478)
XLA Ops:
  0.6 0.0 copy-start
  0.7 0.1 stack.63.place_ref
  0.8 2.1 %edge_rows.1 = (bf16[32,32,128]{2,1,0:T(8,128)(2,1)S(1)}, bf16[4,32,768]{2,1,0:T(8,128)(2,1)S(1)}, bf16[4,32,768]{2,1,0:T(8,128)(2,1)S(1)}, bf16[32,32,768]{2,1,0:T(8,128)(2,1)S(1)}) custom-call(s32[10]{0:T(128)S(1)} %stack.63.place_ref, s32[32,32]{1,0:T(8,128)} %flags_hbm.1, bf16[32,32,768]{2,1,0:T(8,128)(2,1)} %x_hbm.1), custom_call_target="tpu_custom_call" | custom-call | flops 1000000 | bytes 1000000 | tf_op jit(solution)/shard_map/edge_rows/pallas_call | solution.py:490
  2.9 0.5 collective-permute-start.2
  3.4 0.7 %collective-permute-start.3 = (bf16[4,32,768]{2,1,0:T(8,128)(2,1)S(1)}, bf16[4,32,768]{2,1,0:T(8,128)(2,1)S(1)}, u32[]{:S(2)}, u32[]{:S(2)}) collective-permute-start(bf16[4,32,768]{2,1,0:T(8,128)(2,1)S(1)} %get-tuple-element.35), channel_id=1, source_target_pairs={{4,8},{8,4},{5,9},{9,5},{6,10},{10,6},{7,11},{11,7},{20,24},{24,20... | collective-permute-start | bytes 589832 | tf_op jit(solution)/shard_map/ppermute | solution.py:42
  4.1 1.6 %pieces.1 = (bf16[192,768]{1,0:T(8,128)(2,1)S(1)}, bf16[192,768]{1,0:T(8,128)(2,1)S(1)}) custom-call(s32[10]{0:T(128)S(1)} %stack.63.place_ref, bf16[576,768]{1,0:T(8,128)(2,1)} %bitcast.11), custom_call_target="tpu_custom_call" | custom-call | flops 1000000 | bytes 1000000 | tf_op jit(solution)/shard_map/pieces/pallas_call | solution.py:509
  5.7 3.9 %collective-permute-start.1 = (bf16[192,768]{1,0:T(8,128)(2,1)S(1)}, bf16[192,768]{1,0:T(8,128)(2,1)S(1)}, u32[]{:S(2)}, u32[]{:S(2)}) collective-permute-start(bf16[192,768]{1,0:T(8,128)(2,1)S(1)} %get-tuple-element.32), channel_id=1, source_target_pairs={{0,8},{4,12},{8,0},{12,4},{1,9},{5,13},{9,1},{13,5},{2,10},{6,14},... | collective-permute-start | bytes 884744 | tf_op jit(solution)/shard_map/ppermute | solution.py:48
  9.5 0.2 collective-permute-start
  9.7 1.8 %own_norm.1.xq_ref.refs_8_ = bf16[1024,768]{1,0:T(8,128)(2,1)S(1)} custom-call(bf16[32,32,768]{2,1,0:T(8,128)(2,1)S(1)} %get-tuple-element.29.x_ref), custom_call_target="tpu_custom_call" | custom-call | flops 1000000 | bytes 1000000 | tf_op jit(solution)/shard_map/own_norm/pallas_call | solution.py:522
  11.6 0.0 collective-permute-done.2.even_rows_ref
  11.6 0.9 %edge_columns.1 = (bf16[21,8,768]{2,1,0:T(8,128)(2,1)S(1)}, bf16[20,8,768]{2,1,0:T(8,128)(2,1)S(1)}) custom-call(s32[10]{0:T(128)S(1)} %stack.63.place_ref, bf16[32,32,768]{2,1,0:T(8,128)(2,1)S(1)} %get-tuple-element.29.x_ref, bf16[32,32,128]{2,1,0:T(8,128)(2,1)S(1)} %get-tuple-element.34.mark_ref, ...), custom_call_target="tpu_custom_call" | custom-call | flops 1000000 | bytes 2000000 | tf_op jit(solution)/shard_map/edge_columns/pallas_call | solution.py:540
  12.4 2.0 %collective-permute-start.4 = (bf16[21,8,768]{2,1,0:T(8,128)(2,1)S(1)}, bf16[21,8,768]{2,1,0:T(8,128)(2,1)S(1)}, u32[]{:S(2)}, u32[]{:S(2)}) collective-permute-start(bf16[21,8,768]{2,1,0:T(8,128)(2,1)S(1)} %get-tuple-element.36), channel_id=1, source_target_pairs={{0,1},{2,3},{1,0},{3,2},{4,5},{6,7},{5,4},{7,6},{8,9},{10,11},{9,8... | collective-permute-start | bytes 774152 | tf_op jit(solution)/shard_map/ppermute | solution.py:42
  14.5 0.7 %collective-permute-start.5 = (bf16[20,8,768]{2,1,0:T(8,128)(2,1)S(1)}, bf16[20,8,768]{2,1,0:T(8,128)(2,1)S(1)}, u32[]{:S(2)}, u32[]{:S(2)}) collective-permute-start(bf16[20,8,768]{2,1,0:T(8,128)(2,1)S(1)} %get-tuple-element.37), channel_id=1, source_target_pairs={{1,2},{2,1},{5,6},{6,5},{9,10},{10,9},{13,14},{14,13},{17,18},{18,... | collective-permute-start | bytes 737288 | tf_op jit(solution)/shard_map/ppermute | solution.py:42
  15.2 1.3 %collective-permute-start.10 = (bf16[192,768]{1,0:T(8,128)(2,1)S(1)}, bf16[192,768]{1,0:T(8,128)(2,1)S(1)}, u32[]{:S(2)}, u32[]{:S(2)}) collective-permute-start(bf16[192,768]{1,0:T(8,128)(2,1)S(1)} %get-tuple-element.44), channel_id=1, source_target_pairs={{0,8},{4,12},{8,0},{12,4},{1,9},{5,13},{9,1},{13,5},{2,10},{6,14},... | collective-permute-start | bytes 884744 | tf_op jit(solution)/shard_map/ppermute | solution.py:48
  16.5 0.5 collective-permute-done.1.refs_2_
  17.0 4.4 %collective-permute-done.4.got_hbm.even_cols_ref = bf16[21,8,768]{2,1,0:T(8,128)(2,1)S(1)} collective-permute-done((bf16[21,8,768]{2,1,0:T(8,128)(2,1)S(1)}, bf16[21,8,768]{2,1,0:T(8,128)(2,1)S(1)}, u32[]{:S(2)}, u32[]{:S(2)}) %collective-permute-start.4) | collective-permute-done | bytes 258080 | tf_op jit(solution)/shard_map/ppermute | solution.py:42
  21.4 1.7 %collective-permute-start.8 = (bf16[192,768]{1,0:T(8,128)(2,1)S(1)}, bf16[192,768]{1,0:T(8,128)(2,1)S(1)}, u32[]{:S(2)}, u32[]{:S(2)}) collective-permute-start(bf16[192,768]{1,0:T(8,128)(2,1)S(1)} %collective-permute-done.1.refs_2_), channel_id=1, source_target_pairs={{0,16},{16,0},{1,17},{17,1},{2,18},{18,2},{3,19},{19,3},{4,20},{20... | collective-permute-start | bytes 884744 | tf_op jit(solution)/shard_map/ppermute | solution.py:575
  23.1 5.6 %collective-permute-start.6 = (bf16[8,768]{1,0:T(8,128)(2,1)S(1)}, bf16[8,768]{1,0:T(8,128)(2,1)S(1)}, u32[]{:S(2)}, u32[]{:S(2)}) collective-permute-start(bf16[8,768]{1,0:T(8,128)(2,1)S(1)} %carrier_pair.1.refs_0_), channel_id=1, source_target_pairs={{0,2},{1,3},{2,0},{3,1},{4,6},{5,7},{6,4},{7,5},{8,10},{9,11},{10,... | collective-permute-start | bytes 36872 | tf_op jit(solution)/shard_map/ppermute | solution.py:48
  28.6 1.7 %collective-permute-done.6.refs_1_ = bf16[8,768]{1,0:T(8,128)(2,1)S(1)} collective-permute-done((bf16[8,768]{1,0:T(8,128)(2,1)S(1)}, bf16[8,768]{1,0:T(8,128)(2,1)S(1)}, u32[]{:S(2)}, u32[]{:S(2)}) %collective-permute-start.6) | collective-permute-done | bytes 12320 | tf_op jit(solution)/shard_map/ppermute | solution.py:48
  30.3 2.1 %halo_norm.1 = (bf16[1600,768]{1,0:T(8,128)(2,1)S(1)}, f32[16,8,256]{2,1,0:T(8,128)S(1)}) custom-call(s32[10]{0:T(128)S(1)} %stack.63.place_ref, bf16[1024,768]{1,0:T(8,128)(2,1)S(1)} %own_norm.1.xq_ref.refs_8_, bf16[32,32,128]{2,1,0:T(8,128)(2,1)S(1)} %get-tuple-element.34.mark_ref, bf16[4,32,768]{2,1,0:T(8,128)(2,1)S(1)} %collective-permute-done.2.even_rows_ref, ...), custom_call_target="tpu_custom_call" | custom-call | flops 10000000 | bytes 6000000 | tf_op jit(solution)/shard_map/halo_norm/pallas_call | solution.py:596
  32.5 0.1 collective-permute-start.7
  32.5 0.5 collective-permute-start.11
  33.0 0.1 collective-permute-start.9
  33.1 1.0 %final_pack.1.refs_0_ = bf16[208,768]{1,0:T(8,128)(2,1)S(1)} custom-call(bf16[192,768]{1,0:T(8,128)(2,1)} %bitcast.14, bf16[8,768]{1,0:T(8,128)(2,1)S(1)} %carrier_pair.1.refs_0_, bf16[8,768]{1,0:T(8,128)(2,1)S(1)} %collective-permute-done.6.refs_1_), custom_call_target="tpu_custom_call" | custom-call | flops 1000 | bytes 1000 | tf_op jit(solution)/shard_map/final_pack/pallas_call | solution.py:579
  34.1 0.8 %collective-permute-start.13 = (bf16[208,768]{1,0:T(8,128)(2,1)S(1)}, bf16[208,768]{1,0:T(8,128)(2,1)S(1)}, u32[]{:S(2)}, u32[]{:S(2)}) collective-permute-start(bf16[208,768]{1,0:T(8,128)(2,1)S(1)} %final_pack.1.refs_0_), channel_id=1, source_target_pairs={{0,8},{4,12},{8,0},{12,4},{1,9},{5,13},{9,1},{13,5},{2,10},{6,14},... | collective-permute-start | bytes 958472 | tf_op jit(solution)/shard_map/ppermute | solution.py:48
  34.9 0.2 collective-permute-start.12
  35.1 8.2 %project.1 = (bf16[3,1024,256]{2,1,0:T(8,128)(2,1)S(1)}, bf16[3,1600,256]{2,1,0:T(8,128)(2,1)S(1)}, bf16[3,1600,256]{2,1,0:T(8,128)(2,1)S(1)}, bf16[2304,768]{1,0:T(8,128)(2,1)S(1)}) custom-call(s32[10]{0:T(128)S(1)} %stack.63.place_ref, bf16[576,768]{1,0:T(8,128)(2,1)S(1)} %bitcast.13, bf16[576,768]{1,0:T(8,128)(2,1)S(1)} %collective-permute-done.refs_1_, ...), custom_call_target="tpu_custom_call" | custom-call | flops 5000000000 | bytes 14000000 | tf_op jit(solution)/shard_map/project/pallas_call | solution.py:625
  43.3 0.7 %collective-permute-done.13.refs_2_ = bf16[208,768]{1,0:T(8,128)(2,1)S(1)} collective-permute-done((bf16[208,768]{1,0:T(8,128)(2,1)S(1)}, bf16[208,768]{1,0:T(8,128)(2,1)S(1)}, u32[]{:S(2)}, u32[]{:S(2)}) %collective-permute-start.13) | collective-permute-done | bytes 319520 | tf_op jit(solution)/shard_map/ppermute | solution.py:48
  44.0 1.6 %collective-permute-done.14.refs_3_ = bf16[208,768]{1,0:T(8,128)(2,1)S(1)} collective-permute-done((bf16[208,768]{1,0:T(8,128)(2,1)S(1)}, bf16[208,768]{1,0:T(8,128)(2,1)S(1)}, u32[]{:S(2)}, u32[]{:S(2)}) %collective-permute-start.14) | collective-permute-done | bytes 319520 | tf_op jit(solution)/shard_map/ppermute | solution.py:48
  45.7 3.9 %carriers.1 = (bf16[2,2,768]{2,1,0:T(2,128)(2,1)}, bf16[768,768]{1,0:T(8,128)(2,1)S(1)}, bf16[12,256,256]{2,1,0:T(8,128)(2,1)S(1)}, f32[8,768]{1,0:T(8,128)S(1)}) custom-call(s32[10]{0:T(128)S(1)} %stack.63.place_ref, bf16[2304,768]{1,0:T(8,128)(2,1)S(1)} %get-tuple-element.50.wt, bf16[208,768]{1,0:T(8,128)(2,1)S(1)} %final_pack.1.refs_0_, ...), custom_call_target="tpu_custom_call" | custom-call | flops 500000000 | bytes 5000000 | tf_op jit(solution)/shard_map/carriers/pallas_call | solution.py:646
  49.5 6.9 %attend.1.mix_s = bf16[1024,768]{1,0:T(8,128)(2,1)S(1)} custom-call(bf16[3,1024,256]{2,1,0:T(8,128)(2,1)S(1)} %get-tuple-element.46.q_s, bf16[3,1600,256]{2,1,0:T(8,128)(2,1)S(1)} %get-tuple-element.47.k_s, bf16[3,1600,256]{2,1,0:T(8,128)(2,1)S(1)} %get-tuple-element.48.v_s, f32[16,8,256]{2,1,0:T(8,128)S(1)} %get-tuple-element.49.hide_ref, ...), custom_call_target="tpu_custom_call" | custom-call | flops 4000000000 | bytes 12000000 | tf_op jit(solution)/shard_map/attend/pallas_call | solution.py:666
  56.4 2.4 %out.1 = bf16[32,32,768]{2,1,0:T(8,128)(2,1)} custom-call(bf16[32,32,768]{2,1,0:T(8,128)(2,1)S(1)} %get-tuple-element.29.x_ref, bf16[1024,768]{1,0:T(8,128)(2,1)S(1)} %attend.1.mix_s, bf16[768,768]{1,0:T(8,128)(2,1)S(1)} %get-tuple-element.54.wo), custom_call_target="tpu_custom_call" | custom-call | flops 1200000000 | bytes 6000000 | tf_op jit(solution)/shard_map/out/pallas_call | solution.py:681
  (14 shorter events, 0.1 us)
Async XLA Ops:
  0.6 8.9 %copy-start = (bf16[768,576]{0,1:T(8,128)(2,1)S(1)}, bf16[768,576]{0,1:T(8,128)(2,1)}, u32[]{:S(2)}) copy-start(bf16[768,576]{0,1:T(8,128)(2,1)} %param.7) | copy-start | bytes 2654212
  2.9 8.7 %collective-permute-start.2 = (bf16[4,32,768]{2,1,0:T(8,128)(2,1)S(1)}, bf16[4,32,768]{2,1,0:T(8,128)(2,1)S(1)}, u32[]{:S(2)}, u32[]{:S(2)}) collective-permute-start(bf16[4,32,768]{2,1,0:T(8,128)(2,1)S(1)} %get-tuple-element.30), channel_id=1, source_target_pairs={{0,4},{8,12},{4,0},{12,8},{1,5},{9,13},{5,1},{13,9},{2,6},{10,14},... | collective-permute-start | bytes 589832 | tf_op jit(solution)/shard_map/ppermute | solution.py:42
  3.4 8.2 %collective-permute-start.3 = (bf16[4,32,768]{2,1,0:T(8,128)(2,1)S(1)}, bf16[4,32,768]{2,1,0:T(8,128)(2,1)S(1)}, u32[]{:S(2)}, u32[]{:S(2)}) collective-permute-start(bf16[4,32,768]{2,1,0:T(8,128)(2,1)S(1)} %get-tuple-element.35), channel_id=1, source_target_pairs={{4,8},{8,4},{5,9},{9,5},{6,10},{10,6},{7,11},{11,7},{20,24},{24,20... | collective-permute-start | bytes 589832 | tf_op jit(solution)/shard_map/ppermute | solution.py:42
  5.7 11.3 %collective-permute-start.1 = (bf16[192,768]{1,0:T(8,128)(2,1)S(1)}, bf16[192,768]{1,0:T(8,128)(2,1)S(1)}, u32[]{:S(2)}, u32[]{:S(2)}) collective-permute-start(bf16[192,768]{1,0:T(8,128)(2,1)S(1)} %get-tuple-element.32), channel_id=1, source_target_pairs={{0,8},{4,12},{8,0},{12,4},{1,9},{5,13},{9,1},{13,5},{2,10},{6,14},... | collective-permute-start | bytes 884744 | tf_op jit(solution)/shard_map/ppermute | solution.py:48
  9.5 25.5 %collective-permute-start = (bf16[576,768]{1,0:T(8,128)(2,1)S(1)}, bf16[576,768]{1,0:T(8,128)(2,1)S(1)}, u32[]{:S(2)}, u32[]{:S(2)}) collective-permute-start(bf16[576,768]{1,0:T(8,128)(2,1)S(1)} %bitcast.12), channel_id=1, source_target_pairs={{0,4},{4,0},{8,12},{12,8},{1,5},{5,1},{9,13},{13,9},{2,6},{6,2},{1... | collective-permute-start | bytes 2654216 | tf_op jit(solution)/shard_map/ppermute | solution.py:48
  9.7 1.8 %copy-start.1 = (bf16[2,2,768]{2,1,0:T(2,128)(2,1)S(1)}, bf16[2,2,768]{2,1,0:T(2,128)(2,1)}, u32[]{:S(2)}) copy-start(bf16[2,2,768]{2,1,0:T(2,128)(2,1)} %own_ref.1) | copy-start | bytes 18436
  12.4 8.9 %collective-permute-start.4 = (bf16[21,8,768]{2,1,0:T(8,128)(2,1)S(1)}, bf16[21,8,768]{2,1,0:T(8,128)(2,1)S(1)}, u32[]{:S(2)}, u32[]{:S(2)}) collective-permute-start(bf16[21,8,768]{2,1,0:T(8,128)(2,1)S(1)} %get-tuple-element.36), channel_id=1, source_target_pairs={{0,1},{2,3},{1,0},{3,2},{4,5},{6,7},{5,4},{7,6},{8,9},{10,11},{9,8... | collective-permute-start | bytes 774152 | tf_op jit(solution)/shard_map/ppermute | solution.py:42
  14.5 2.5 %collective-permute-start.5 = (bf16[20,8,768]{2,1,0:T(8,128)(2,1)S(1)}, bf16[20,8,768]{2,1,0:T(8,128)(2,1)S(1)}, u32[]{:S(2)}, u32[]{:S(2)}) collective-permute-start(bf16[20,8,768]{2,1,0:T(8,128)(2,1)S(1)} %get-tuple-element.37), channel_id=1, source_target_pairs={{1,2},{2,1},{5,6},{6,5},{9,10},{10,9},{13,14},{14,13},{17,18},{18,... | collective-permute-start | bytes 737288 | tf_op jit(solution)/shard_map/ppermute | solution.py:42
  15.2 17.4 %collective-permute-start.10 = (bf16[192,768]{1,0:T(8,128)(2,1)S(1)}, bf16[192,768]{1,0:T(8,128)(2,1)S(1)}, u32[]{:S(2)}, u32[]{:S(2)}) collective-permute-start(bf16[192,768]{1,0:T(8,128)(2,1)S(1)} %get-tuple-element.44), channel_id=1, source_target_pairs={{0,8},{4,12},{8,0},{12,4},{1,9},{5,13},{9,1},{13,5},{2,10},{6,14},... | collective-permute-start | bytes 884744 | tf_op jit(solution)/shard_map/ppermute | solution.py:48
  21.4 11.6 %collective-permute-start.8 = (bf16[192,768]{1,0:T(8,128)(2,1)S(1)}, bf16[192,768]{1,0:T(8,128)(2,1)S(1)}, u32[]{:S(2)}, u32[]{:S(2)}) collective-permute-start(bf16[192,768]{1,0:T(8,128)(2,1)S(1)} %collective-permute-done.1.refs_2_), channel_id=1, source_target_pairs={{0,16},{16,0},{1,17},{17,1},{2,18},{18,2},{3,19},{19,3},{4,20},{20... | collective-permute-start | bytes 884744 | tf_op jit(solution)/shard_map/ppermute | solution.py:575
  23.1 7.2 %collective-permute-start.6 = (bf16[8,768]{1,0:T(8,128)(2,1)S(1)}, bf16[8,768]{1,0:T(8,128)(2,1)S(1)}, u32[]{:S(2)}, u32[]{:S(2)}) collective-permute-start(bf16[8,768]{1,0:T(8,128)(2,1)S(1)} %carrier_pair.1.refs_0_), channel_id=1, source_target_pairs={{0,2},{1,3},{2,0},{3,1},{4,6},{5,7},{6,4},{7,5},{8,10},{9,11},{10,... | collective-permute-start | bytes 36872 | tf_op jit(solution)/shard_map/ppermute | solution.py:48
  32.5 2.5 %collective-permute-start.7 = (bf16[192,768]{1,0:T(8,128)(2,1)S(1)}, bf16[192,768]{1,0:T(8,128)(2,1)S(1)}, u32[]{:S(2)}, u32[]{:S(2)}) collective-permute-start(bf16[192,768]{1,0:T(8,128)(2,1)S(1)} %collective-permute-done.1.refs_2_), channel_id=1, source_target_pairs={{0,4},{4,0},{8,12},{12,8},{1,5},{5,1},{9,13},{13,9},{2,6},{6,2},{1... | collective-permute-start | bytes 884744 | tf_op jit(solution)/shard_map/ppermute | solution.py:48
  32.5 2.5 %collective-permute-start.11 = (bf16[192,768]{1,0:T(8,128)(2,1)S(1)}, bf16[192,768]{1,0:T(8,128)(2,1)S(1)}, u32[]{:S(2)}, u32[]{:S(2)}) collective-permute-start(bf16[192,768]{1,0:T(8,128)(2,1)S(1)} %collective-permute-done.10.refs_6_), channel_id=1, source_target_pairs={{0,4},{4,0},{8,12},{12,8},{1,5},{5,1},{9,13},{13,9},{2,6},{6,2},{1... | collective-permute-start | bytes 884744 | tf_op jit(solution)/shard_map/ppermute | solution.py:48
  33.0 2.1 %collective-permute-start.9 = (bf16[192,768]{1,0:T(8,128)(2,1)S(1)}, bf16[192,768]{1,0:T(8,128)(2,1)S(1)}, u32[]{:S(2)}, u32[]{:S(2)}) collective-permute-start(bf16[192,768]{1,0:T(8,128)(2,1)S(1)} %collective-permute-done.8.refs_4_), channel_id=1, source_target_pairs={{0,4},{4,0},{8,12},{12,8},{1,5},{5,1},{9,13},{13,9},{2,6},{6,2},{1... | collective-permute-start | bytes 884744 | tf_op jit(solution)/shard_map/ppermute | solution.py:48
  34.1 9.9 %collective-permute-start.13 = (bf16[208,768]{1,0:T(8,128)(2,1)S(1)}, bf16[208,768]{1,0:T(8,128)(2,1)S(1)}, u32[]{:S(2)}, u32[]{:S(2)}) collective-permute-start(bf16[208,768]{1,0:T(8,128)(2,1)S(1)} %final_pack.1.refs_0_), channel_id=1, source_target_pairs={{0,8},{4,12},{8,0},{12,4},{1,9},{5,13},{9,1},{13,5},{2,10},{6,14},... | collective-permute-start | bytes 958472 | tf_op jit(solution)/shard_map/ppermute | solution.py:48
  34.9 9.1 %collective-permute-start.12 = (bf16[208,768]{1,0:T(8,128)(2,1)S(1)}, bf16[208,768]{1,0:T(8,128)(2,1)S(1)}, u32[]{:S(2)}, u32[]{:S(2)}) collective-permute-start(bf16[208,768]{1,0:T(8,128)(2,1)S(1)} %final_pack.1.refs_0_), channel_id=1, source_target_pairs={{0,4},{4,0},{8,12},{12,8},{1,5},{5,1},{9,13},{13,9},{2,6},{6,2},{1... | collective-permute-start | bytes 958472 | tf_op jit(solution)/shard_map/ppermute | solution.py:48
  44.0 1.6 %collective-permute-start.14 = (bf16[208,768]{1,0:T(8,128)(2,1)S(1)}, bf16[208,768]{1,0:T(8,128)(2,1)S(1)}, u32[]{:S(2)}, u32[]{:S(2)}) collective-permute-start(bf16[208,768]{1,0:T(8,128)(2,1)S(1)} %collective-permute-done.13.refs_2_), channel_id=1, source_target_pairs={{0,4},{4,0},{8,12},{12,8},{1,5},{5,1},{9,13},{13,9},{2,6},{6,2},{1... | collective-permute-start | bytes 958472 | tf_op jit(solution)/shard_map/ppermute | solution.py:48
where the time goes:
time: 59 us; the launch traced here: 58.7 us
  Pallas kernels  30.8 us (52%)
  starting transfers between devices  18.1 us (31%)
  waiting for transfers between devices  8.91 us (15%)
  between operations  0.83 us (1%)
    ppermute x10, starting transfers between devices, swapped(): return lax.ppermute(block, axis, [(i, i ^ bit) for i in range(count)])  12.6 us
    pallas_call x1, Pallas kernels, local(): pl.pallas_call(functools.partial(project_kernel, offsets, numbered, tripl...  8.23 us
    pallas_call x1, Pallas kernels, local(): pl.pallas_call(functools.partial(attend_kernel, rows // TILE, cols // TIL...  6.85 us
    ppermute x10, waiting for transfers between devices, swapped(): return lax.ppermute(block, axis, [(i, i ^ bit) for i in range(count)])  4.53 us
    ppermute x4, waiting for transfers between devices, pair_swapped(): got.append(lax.ppermute(block, axis, pairs + [(b, a) for a, b in pairs]))  4.38 us
    ppermute x4, starting transfers between devices, pair_swapped(): got.append(lax.ppermute(block, axis, pairs + [(b, a) for a, b in pairs]))  3.88 us
    pallas_call x1, Pallas kernels, local(): pl.pallas_call(functools.partial(carrier_kernel, offsets), out_shape=(jax...  3.86 us
    pallas_call x1, Pallas kernels, local(): pl.pallas_call(out_kernel, out_shape=jax.ShapeDtypeStruct(grid_elements.s...  2.36 us
  transfers between devices with their start and end apart: 15, of which 5 were waited for; matrix products, arithmetic and copies ran while one was open for 0% of the time, Pallas kernels for 27%

commit v1 on v0

--- a/solution.py
+++ b/solution.py
@@ -65,13 +65,20 @@
     return jnp.concatenate([first, lines[:, :, LANES:]], axis=2)
 
 
-def edge_kernel(place_ref, flags_hbm, x_hbm, mark_ref, even_ref, odd_ref, x_ref, *scratch):
-    flags_ref, spread, sems = scratch
-    rows, cols = flags_ref.shape
+def edge_kernel(place_ref, flags_hbm, x_hbm, carriers_ref, mark_ref, *refs):
+    even_rows_ref, odd_rows_ref, even_cols_ref, odd_cols_ref, x_ref, flags_ref, spread, carriers_s, sems = refs
+    rows, cols, channels = x_ref.shape
+    middle = rows // 2
     flags_copy = pltpu.make_async_copy(flags_hbm, flags_ref, sems.at[0])
     x_copy = pltpu.make_async_copy(x_hbm, x_ref, sems.at[1])
     flags_copy.start()
     x_copy.start()
+    per_row = carriers_ref.shape[1]
+    carriers_s[...] = jnp.zeros_like(carriers_s)
+    for i in range(carriers_ref.shape[0]):
+        carriers_s[i * per_row : (i + 1) * per_row, :] = carriers_ref[i].astype(jnp.float32)
+    for i in range(carriers_s.shape[0] // TILE):
+        even_cols_ref[middle + i] = carriers_s[i * TILE : (i + 1) * TILE, :].astype(jnp.bfloat16)
     flags_copy.wait()
     row_at = lax.broadcasted_iota(jnp.int32, (cols, cols), 0)
     diagonal = row_at == lax.broadcasted_iota(jnp.int32, (cols, cols), 1)
@@ -86,8 +93,24 @@
         for at in (slice(0, RADIUS), slice(rows - RADIUS, rows))
     ]
     even = place_ref[EVEN_ROW] > 0
-    even_ref[...] = jnp.where(even, last, first).astype(jnp.bfloat16)
-    odd_ref[...] = jnp.where(even, first, last).astype(jnp.bfloat16)
+    even_rows_ref[...] = jnp.where(even, last, first).astype(jnp.bfloat16)
+    odd_rows_ref[...] = jnp.where(even, first, last).astype(jnp.bfloat16)
+    even = place_ref[EVEN_COL] > 0
+    low = lax.broadcasted_iota(jnp.int32, (1, TILE, 1), 1) < RADIUS
+    for lane in range(0, channels, LANES):
+        lanes = slice(lane, lane + LANES)
+        strips = []
+        for columns in (slice(0, TILE), slice(cols - TILE, cols)):
+            halves = []
+            for part in (slice(0, middle), slice(middle, rows)):
+                lines = x_ref[part, columns, lanes].astype(jnp.float32)
+                halves.append(jnp.where(marks[part, columns, :] > INVALID / 2, INVALID, lines) if lane == 0 else lines)
+            strips.append(halves)
+        (first_up, first_down), (last_up, last_down) = strips
+        first = jnp.where(low, first_up, jnp.roll(first_down, RADIUS, axis=1))
+        last = jnp.where(low, jnp.roll(last_up, RADIUS, axis=1), last_down)
+        even_cols_ref[:middle, :, lanes] = jnp.where(even, last, first).astype(jnp.bfloat16)
+        odd_cols_ref[:, :, lanes] = jnp.where(even, first, last).astype(jnp.bfloat16)
 
 
 def piece_kernel(place_ref, triple_hbm, mine_ref, last_ref, sems):
@@ -103,41 +126,17 @@
         copy.wait()
 
 
-def strip_kernel(place_ref, x_ref, mark_ref, even_rows_ref, odd_rows_ref, carriers_ref, even_ref, odd_ref, carriers_s):
-    per_row = carriers_ref.shape[1]
-    carriers_s[...] = jnp.zeros_like(carriers_s)
-    for i in range(carriers_ref.shape[0]):
-        carriers_s[i * per_row : (i + 1) * per_row, :] = carriers_ref[i].astype(jnp.float32)
-    for i in range(carriers_s.shape[0] // TILE):
-        even_ref[odd_ref.shape[0] + i] = carriers_s[i * TILE : (i + 1) * TILE, :].astype(jnp.bfloat16)
-    rows, cols, channels = x_ref.shape
-    middle = rows // 2
+def corner_kernel(place_ref, even_rows_ref, odd_rows_ref, even_ref, odd_ref):
+    cols = even_rows_ref.shape[1]
     low = lax.broadcasted_iota(jnp.int32, (1, TILE, 1), 1) < RADIUS
-    even_row, even_col = place_ref[EVEN_ROW] > 0, place_ref[EVEN_COL] > 0
-    for lane in range(0, channels, LANES):
-        lanes = slice(lane, lane + LANES)
-        strips = []
-        for columns, last in ((slice(0, TILE), False), (slice(cols - TILE, cols), True)):
-
-            def own(part):
-                lines = x_ref[part, columns, lanes].astype(jnp.float32)
-                if lane == 0:
-                    lines = jnp.where(mark_ref[part, columns, :].astype(jnp.float32) > INVALID / 2, INVALID, lines)
-                return lines
-
-            even_rows = even_rows_ref[:, columns, lanes].astype(jnp.float32)
-            odd_rows = odd_rows_ref[:, columns, lanes].astype(jnp.float32)
-            top, bottom = jnp.where(even_row, odd_rows, even_rows), jnp.where(even_row, even_rows, odd_rows)
-            upper = jnp.concatenate([top, own(slice(0, middle))], axis=0)
-            lower = jnp.concatenate([own(slice(middle, rows)), bottom], axis=0)
-            if last:
-                upper = jnp.roll(upper, RADIUS, axis=1)
-            else:
-                lower = jnp.roll(lower, RADIUS, axis=1)
-            strips.append(jnp.where(low, upper, lower))
-        first, last = strips
-        even_ref[: odd_ref.shape[0], :, lanes] = jnp.where(even_col, last, first).astype(jnp.bfloat16)
-        odd_ref[:, :, lanes] = jnp.where(even_col, first, last).astype(jnp.bfloat16)
+    flip = place_ref[EVEN_ROW] > 0
+    even_rows, odd_rows = even_rows_ref[...].astype(jnp.float32), odd_rows_ref[...].astype(jnp.float32)
+    top, bottom = jnp.where(flip, odd_rows, even_rows), jnp.where(flip, even_rows, odd_rows)
+    first = jnp.where(low, top[:, :TILE, :], jnp.roll(bottom[:, :TILE, :], RADIUS, axis=1))
+    last = jnp.where(low, jnp.roll(top[:, cols - TILE :, :], RADIUS, axis=1), bottom[:, cols - TILE :, :])
+    even = place_ref[EVEN_COL] > 0
+    even_ref[...] = jnp.where(even, last, first).astype(jnp.bfloat16)
+    odd_ref[...] = jnp.where(even, first, last).astype(jnp.bfloat16)
 
 
 def carrier_pair_kernel(own_ref, got_hbm, out_ref, got_s, pair_s, sem):
@@ -152,14 +151,12 @@
     out_ref[...] = pair_s[...].astype(jnp.bfloat16)
 
 
-def pack_kernel(final_hbm, *refs):
-    parts, (out_ref, sem) = refs[:-2], refs[-2:]
-    rows = final_hbm.shape[0]
-    copy = pltpu.make_async_copy(final_hbm, out_ref.at[0:rows, :], sem)
-    copy.start()
+def pack_kernel(final_ref, *refs):
+    parts, out_ref = refs[:-1], refs[-1]
+    rows = final_ref.shape[0]
+    out_ref[:rows, :] = final_ref[...]
     carriers = jnp.concatenate([part[...].astype(jnp.float32) for part in parts], axis=0)
     out_ref[rows:, :] = carriers.astype(jnp.bfloat16)
-    copy.wait()
 
 
 def own_kernel(x_ref, xq_ref):
@@ -178,15 +175,19 @@
     lax.fori_loop(0, rows // step, own, 0)
 
 
-def halo_kernel(place_ref, xq_ref, mark_ref, even_rows_ref, odd_rows_ref, even_cols_ref, odd_cols_ref, xkv_ref, hide_ref, *scratch):
+def halo_kernel(place_ref, xq_ref, mark_ref, *refs):
+    even_rows_ref, odd_rows_ref, even_cols_ref, odd_cols_ref, even_corners_ref, odd_corners_ref, xkv_ref, hide_ref = refs[:8]
+    scratch = refs[8:]
     rows, cols, _ = mark_ref.shape
     wide_rows, wide_cols = rows + 2 * RADIUS, cols + 2 * RADIUS
     half = wide_rows // 2
     step = 2
-    top_s, bottom_s, left_s, right_s, top_ref, bottom_ref, left_ref, right_ref, flag_s = scratch
+    top_s, bottom_s, left_s, right_s, left_corner_s, right_corner_s = scratch[:6]
+    top_ref, bottom_ref, left_ref, right_ref, left_corner_ref, right_corner_ref, flag_s = scratch[6:]
     for even, odd, low, high, low_flags, high_flags, parity, size in (
         (even_rows_ref, odd_rows_ref, top_s, bottom_s, top_ref, bottom_ref, EVEN_ROW, 2),
-        (even_cols_ref, odd_cols_ref, left_s, right_s, left_ref, right_ref, EVEN_COL, 5),
+        (even_cols_ref, odd_cols_ref, left_s, right_s, left_ref, right_ref, EVEN_COL, 4),
+        (even_corners_ref, odd_corners_ref, left_corner_s, right_corner_s, left_corner_ref, right_corner_ref, EVEN_COL, 4),
     ):
         flip = place_ref[parity] > 0
         for i in range(0, odd.shape[0], size):
@@ -209,33 +210,23 @@
             to_ref[pl.ds(to, step * TILE), :] = lines.astype(jnp.bfloat16)
             before = after
 
-    def sides(at, upper, left_ref, right_ref, lanes):
+    def sides(at, upper, left_ref, right_ref):
+        left, right = lines_of(left_ref[pl.ds(at, step)]), lines_of(right_ref[pl.ds(at, step)])
         if upper:
-            at = at - half
-            left, right = jnp.roll(lines_of(left_ref[pl.ds(at, step), :, lanes]), RADIUS, axis=1), lines_of(
-                right_ref[pl.ds(at, step), :, lanes]
-            )
-        else:
-            left, right = lines_of(left_ref[pl.ds(at, step), :, lanes]), jnp.roll(
-                lines_of(right_ref[pl.ds(at, step), :, lanes]), RADIUS, axis=1
-            )
-        return left, right
-
-    every, few = slice(None), slice(0, LANES)
+            return jnp.roll(left, RADIUS, axis=1), right
+        return left, jnp.roll(right, RADIUS, axis=1)
 
     def hide_if(border, lines):
         return jnp.where(place_ref[border] > 0, INVALID, lines)
 
-    def mark_sides(at, upper):
-        left, right = sides(at, upper, left_ref, right_ref, few)
-        return hide_if(2, left), hide_if(3, right)
-
     def band(at, ref, ref_s, first, upper):
         cut = [slice(c * TILE, (c + 1) * TILE) for c in range(cols // TILE)]
-        merge(at, [ref_s[first : first + step, k, :] for k in cut], *sides(at, upper, left_s, right_s, every), xkv_ref)
+        lines = ref_s[first : first + step]
+        merge(at, [lines[:, k, :] for k in cut], *sides(first, upper, left_corner_s, right_corner_s), xkv_ref)
         marks = hide_if(int(upper), ref[first : first + step])
-        beside = [hide_if(int(upper), side) for side in mark_sides(at, upper)]
-        merge(at, [marks[:, k, :] for k in cut], *beside, flag_s)
+        left, right = sides(first, upper, left_corner_ref, right_corner_ref)
+        left, right = hide_if(int(upper), hide_if(2, left)), hide_if(int(upper), hide_if(3, right))
+        merge(at, [marks[:, k, :] for k in cut], left, right, flag_s)
 
     for i in range(0, RADIUS, step):
         band(i, top_ref, top_s, i, False)
@@ -248,10 +239,12 @@
         for c in range(cols // TILE):
             first = pl.multiple_of(c * rows * TILE + own * TILE, step * TILE)
             blocks.append(xq_ref[pl.ds(first, step * TILE), :].astype(jnp.float32).reshape(step, TILE, -1))
-        merge(at, blocks, *sides(at, upper, left_s, right_s, every), xkv_ref)
+        strip_at = own - (rows // 2 if upper else 0)
+        merge(at, blocks, *sides(strip_at, upper, left_s, right_s), xkv_ref)
         marks = mark_ref[pl.ds(own, step)].astype(jnp.float32)
         marks = [marks[:, c * TILE : (c + 1) * TILE, :] for c in range(cols // TILE)]
-        merge(at, marks, *mark_sides(at, upper), flag_s)
+        left, right = sides(strip_at, upper, left_ref, right_ref)
+        merge(at, marks, hide_if(2, left), hide_if(3, right), flag_s)
         return 0
 
     lax.fori_loop(RADIUS // step, half // step, lambda i, _: middle(i, False), 0)
@@ -475,7 +468,10 @@
     hbm = pl.BlockSpec(memory_space=pltpu.HBM)
     small = pltpu.CompilerParams(vmem_limit_bytes=8 * 1024 * 1024)
     row_strip = jax.ShapeDtypeStruct((RADIUS, cols, channels), jnp.bfloat16)
-    col_strip = jax.ShapeDtypeStruct((wide_rows // 2, 2 * RADIUS, channels), jnp.bfloat16)
+    col_strip = jax.ShapeDtypeStruct((rows // 2, TILE, channels), jnp.bfloat16)
+    corner = jax.ShapeDtypeStruct((RADIUS, TILE, channels), jnp.bfloat16)
+    own_rows = summary_vectors.shape[0] * summary_vectors.shape[1]
+    carrier_tiles = -(-own_rows // TILE)
 
     row, col, img = lax.axis_size("row"), lax.axis_size("col"), lax.axis_size("img")
     row_at, col_at, img_at = lax.axis_index("row"), lax.axis_index("col"), lax.axis_index("img")
@@ -487,25 +483,28 @@
     place = [row_at == 0, row_at == row - 1, col_at == 0, col_at == col - 1, row_at % 2 == 0, col_at % 2 == 0, row_at]
     place = jnp.stack([jnp.asarray(p).astype(jnp.int32) for p in place + [start * piece_rows for start in starts]])
 
-    mark, even_rows, odd_rows, x = pl.pallas_call(
+    mark, even_rows, odd_rows, even_cols, odd_cols, x = pl.pallas_call(
         edge_kernel,
         out_shape=(
             pltpu.VMEM((rows, cols, LANES), jnp.bfloat16),
             pltpu.VMEM(row_strip.shape, jnp.bfloat16),
             pltpu.VMEM(row_strip.shape, jnp.bfloat16),
+            pltpu.VMEM((col_strip.shape[0] + carrier_tiles, *col_strip.shape[1:]), jnp.bfloat16),
+            pltpu.VMEM(col_strip.shape, jnp.bfloat16),
             pltpu.VMEM(grid_elements.shape, jnp.bfloat16),
         ),
-        in_specs=[scalars, hbm, hbm],
-        out_specs=(vmem,) * 4,
+        in_specs=[scalars, hbm, hbm, vmem],
+        out_specs=(vmem,) * 6,
         scratch_shapes=[
             pltpu.VMEM((rows, cols), jnp.int32),
             pltpu.VMEM((rows * cols, cols), jnp.bfloat16),
+            pltpu.VMEM((carrier_tiles * TILE, channels), jnp.float32),
             pltpu.SemaphoreType.DMA((2,)),
         ],
         compiler_params=small,
         cost_estimate=pl.CostEstimate(flops=1_000_000, bytes_accessed=1_000_000, transcendentals=0),
         name="edge_rows",
-    )(place, *(pltpu.with_memory_space_constraint(a, pltpu.HBM) for a in (genuine_flags, grid_elements)))
+    )(place, *(pltpu.with_memory_space_constraint(a, pltpu.HBM) for a in (genuine_flags, grid_elements)), summary_vectors)
     mine, last = pl.pallas_call(
         piece_kernel,
         out_shape=(
@@ -529,28 +528,24 @@
         name="own_norm",
     )(x)
     even_rows, odd_rows = pair_swapped(even_rows, odd_rows, "row")
+    even_cols, odd_cols = pair_swapped(even_cols, odd_cols, "col")
 
     far_pieces = []
     if relays:
         first = swapped(mine, "row", far)
     far_last = swapped(after(last, even_rows, odd_rows), "row", far)
 
-    own_rows = summary_vectors.shape[0] * summary_vectors.shape[1]
-    carrier_tiles = -(-own_rows // TILE)
-    even_cols, odd_cols = pl.pallas_call(
-        strip_kernel,
-        out_shape=(
-            pltpu.VMEM((col_strip.shape[0] + carrier_tiles, *col_strip.shape[1:]), jnp.bfloat16),
-            pltpu.VMEM(col_strip.shape, jnp.bfloat16),
-        ),
-        in_specs=[scalars] + [vmem] * 5,
+    even_corners, odd_corners = pl.pallas_call(
+        corner_kernel,
+        out_shape=(pltpu.VMEM(corner.shape, jnp.bfloat16),) * 2,
+        in_specs=[scalars] + [vmem] * 2,
         out_specs=(vmem,) * 2,
-        scratch_shapes=[pltpu.VMEM((carrier_tiles * TILE, channels), jnp.float32)],
         compiler_params=small,
-        cost_estimate=pl.CostEstimate(flops=1_000_000, bytes_accessed=2_000_000, transcendentals=0),
-        name="edge_columns",
-    )(place, x, after(mark, xq), even_rows, odd_rows, summary_vectors)
-    even_cols, odd_cols = pair_swapped(even_cols, odd_cols, "col")
+        cost_estimate=pl.CostEstimate(flops=1_000_000, bytes_accessed=1_000_000, transcendentals=0),
+        name="corners",
+    )(place, after(even_rows, xq), after(odd_rows, even_cols, odd_cols))
+    even_corners, odd_corners = pair_swapped(even_corners, odd_corners, "col")
+
     carriers = pl.pallas_call(
         carrier_pair_kernel,
         out_shape=pltpu.VMEM((2 * own_rows, channels), jnp.bfloat16),
@@ -568,7 +563,7 @@
     parts = [carriers]
     for bit in bits_of(col)[:-1]:
         carriers = carriers if len(parts) == 1 else jnp.concatenate(parts, axis=0)
-        got = swapped(carriers, "col", bit)
+        got = swapped(carriers, "col", 2 * bit - 1)
         parts.append(got)
     if relays:
         first = after(first, even_cols, odd_cols)
@@ -579,37 +574,37 @@
     final_pack = pl.pallas_call(
         pack_kernel,
         out_shape=pltpu.VMEM((final_t.shape[0] + col * own_rows, channels), jnp.bfloat16),
-        in_specs=[hbm] + [vmem] * len(parts),
+        in_specs=[vmem] * (1 + len(parts)),
         out_specs=vmem,
-        scratch_shapes=[pltpu.SemaphoreType.DMA],
         compiler_params=small,
         cost_estimate=pl.CostEstimate(flops=1_000, bytes_accessed=1_000, transcendentals=0),
         name="final_pack",
-    )(pltpu.with_memory_space_constraint(final_t, pltpu.HBM), *parts)
-    finals, triples, offsets = [final_pack], [triple_t], [0]
+    )(final_t, *parts)
+    finals, triples, offsets = [final_pack], [after(triple_t, even_cols, odd_cols, even_rows, odd_rows, xq)], [0]
     for bit in rest:
         finals = finals + [swapped(p, "row", bit) for p in finals]
         triples = triples + [swapped(p, "row", bit) for p in triples]
         offsets = offsets + [o ^ bit for o in offsets]
     tiles = (rows // TILE) * (cols // TILE)
     keys = 4 * TILE * TILE
+    strips = [row_strip] * 2 + [col_strip] * 2 + [corner] * 2
     xkv, hide = pl.pallas_call(
         halo_kernel,
         out_shape=(
             pltpu.VMEM((wide_rows * wide_cols, channels), jnp.bfloat16),
             pltpu.VMEM((tiles, 8, keys), jnp.float32),
         ),
-        in_specs=[scalars] + [vmem] * 6,
+        in_specs=[scalars] + [vmem] * 8,
         out_specs=(vmem,) * 2,
         scratch_shapes=[
-            *[pltpu.VMEM(shape.shape, jnp.float32) for shape in (row_strip, row_strip, col_strip, col_strip)],
-            *[pltpu.VMEM((*shape.shape[:2], LANES), jnp.float32) for shape in (row_strip, row_strip, col_strip, col_strip)],
+            *[pltpu.VMEM(shape.shape, jnp.float32) for shape in strips],
+            *[pltpu.VMEM((*shape.shape[:2], LANES), jnp.float32) for shape in strips],
             pltpu.VMEM((wide_rows * wide_cols, LANES), jnp.bfloat16),
         ],
         compiler_params=pltpu.CompilerParams(vmem_limit_bytes=12 * 1024 * 1024),
         cost_estimate=pl.CostEstimate(flops=10_000_000, bytes_accessed=6_000_000, transcendentals=1000),
         name="halo_norm",
-    )(place, after(xq, got), mark, even_rows, odd_rows, even_cols, odd_cols)
+    )(place, after(xq, got), mark, even_rows, odd_rows, even_cols, odd_cols, even_corners, odd_corners)
 
     far_final = swapped(final_pack, "row", far)
 

time: 59 us -> 63.7 us (1.080)
  the two profiles are of different devices: /device:TPU:0 before, /device:TPU:9 now
where the time goes in v1:
time: 63.7 us; the launch traced here: 63.4 us
  Pallas kernels  29.9 us (47%)
  starting transfers between devices  20.5 us (32%)
  waiting for transfers between devices  11.3 us (18%)
  between operations  0.89 us (1%)
  local copies, waits for them, and re-layouts  0.8 us (1%)
    ppermute x6, starting transfers between devices, pair_swapped(): got.append(lax.ppermute(block, axis, pairs + [(b, a) for a, b in pairs]))  10.9 us
    ppermute x10, starting transfers between devices, swapped(): return lax.ppermute(block, axis, [(i, i ^ bit) for i in range(count)])  8.46 us
    ppermute x10, waiting for transfers between devices, swapped(): return lax.ppermute(block, axis, [(i, i ^ bit) for i in range(count)])  8.33 us
    pallas_call x1, Pallas kernels, local(): pl.pallas_call(functools.partial(project_kernel, offsets, numbered, tripl...  8.2 us
    pallas_call x1, Pallas kernels, local(): pl.pallas_call(functools.partial(attend_kernel, rows // TILE, cols // TIL...  6.98 us
    pallas_call x1, Pallas kernels, local(): pl.pallas_call(functools.partial(carrier_kernel, offsets), out_shape=(jax...  3.86 us
    ppermute x6, waiting for transfers between devices, pair_swapped(): got.append(lax.ppermute(block, axis, pairs + [(b, a) for a, b in pairs]))  2.94 us
    pallas_call x1, Pallas kernels, local(): pl.pallas_call(out_kernel, out_shape=jax.ShapeDtypeStruct(grid_elements.s...  2.35 us
  transfers between devices with their start and end apart: 17, of which 6 were waited for; matrix products, arithmetic and copies ran while one was open for 0% of the time, Pallas kernels for 23%

profile of v1, /device:TPU:9, one launch (start us, length us, event | category | flops | bytes accessed | tf_op | source)
XLA Modules:
  0.0 63.4 jit_solution(11208685136857186885)
XLA Ops:
  0.7 0.1 stack.63.place_ref
  0.8 0.7 %copy-done.2 = bf16[2,2,768]{2,1,0:T(2,128)(2,1)S(1)} copy-done((bf16[2,2,768]{2,1,0:T(2,128)(2,1)S(1)}, bf16[2,2,768]{2,1,0:T(2,128)(2,1)}, u32[]{:S(2)}) %copy-start.2) | copy-done | bytes 6168
  1.5 2.3 %edge_rows.1 = (bf16[32,32,128]{2,1,0:T(8,128)(2,1)S(1)}, bf16[4,32,768]{2,1,0:T(8,128)(2,1)S(1)}, bf16[4,32,768]{2,1,0:T(8,128)(2,1)S(1)}, bf16[17,8,768]{2,1,0...) custom-call(s32[10]{0:T(128)S(1)} %stack.63.place_ref, s32[32,32]{1,0:T(8,128)} %flags_hbm.1, ...), custom_call_target="tpu_custom_call" | custom-call | flops 1000000 | bytes 1000000 | tf_op jit(solution)/shard_map/edge_rows/pallas_call | solution.py:486
  3.7 0.1 collective-permute-start
  3.8 4.5 %collective-permute-start.1 = (bf16[16,8,768]{2,1,0:T(8,128)(2,1)S(1)}, bf16[16,8,768]{2,1,0:T(8,128)(2,1)S(1)}, u32[]{:S(2)}, u32[]{:S(2)}) collective-permute-start(bf16[16,8,768]{2,1,0:T(8,128)(2,1)S(1)} %get-tuple-element.35), channel_id=1, source_target_pairs={{1,2},{2,1},{5,6},{6,5},{9,10},{10,9},{13,14},{14,13},{17,18},{18,... | collective-permute-start | bytes 589832 | tf_op jit(solution)/shard_map/ppermute | solution.py:42
  8.3 4.3 %collective-permute-start.3 = (bf16[4,32,768]{2,1,0:T(8,128)(2,1)S(1)}, bf16[4,32,768]{2,1,0:T(8,128)(2,1)S(1)}, u32[]{:S(2)}, u32[]{:S(2)}) collective-permute-start(bf16[4,32,768]{2,1,0:T(8,128)(2,1)S(1)} %get-tuple-element.37), channel_id=1, source_target_pairs={{4,8},{8,4},{5,9},{9,5},{6,10},{10,6},{7,11},{11,7},{20,24},{24,20... | collective-permute-start | bytes 589832 | tf_op jit(solution)/shard_map/ppermute | solution.py:42
  12.6 0.1 collective-permute-start.2
  12.6 1.6 %pieces.1 = (bf16[192,768]{1,0:T(8,128)(2,1)S(1)}, bf16[192,768]{1,0:T(8,128)(2,1)S(1)}) custom-call(s32[10]{0:T(128)S(1)} %stack.63.place_ref, bf16[576,768]{1,0:T(8,128)(2,1)} %bitcast.11), custom_call_target="tpu_custom_call" | custom-call | flops 1000000 | bytes 1000000 | tf_op jit(solution)/shard_map/pieces/pallas_call | solution.py:508
  14.3 0.2 collective-permute-start.5
  14.5 1.8 %own_norm.1.xq_ref.refs_8_ = bf16[1024,768]{1,0:T(8,128)(2,1)S(1)} custom-call(bf16[32,32,768]{2,1,0:T(8,128)(2,1)S(1)} %get-tuple-element.33.x_ref), custom_call_target="tpu_custom_call" | custom-call | flops 1000000 | bytes 1000000 | tf_op jit(solution)/shard_map/own_norm/pallas_call | solution.py:521
  16.3 0.5 collective-permute-start.4
  16.8 1.7 %collective-permute-start.12 = (bf16[192,768]{1,0:T(8,128)(2,1)S(1)}, bf16[192,768]{1,0:T(8,128)(2,1)S(1)}, u32[]{:S(2)}, u32[]{:S(2)}) collective-permute-start(bf16[192,768]{1,0:T(8,128)(2,1)S(1)} %get-tuple-element.52), channel_id=1, source_target_pairs={{0,8},{4,12},{8,0},{12,4},{1,9},{5,13},{9,1},{13,5},{2,10},{6,14},... | collective-permute-start | bytes 884744 | tf_op jit(solution)/shard_map/ppermute | solution.py:48
  18.5 3.9 %collective-permute-done.5.refs_2_ = bf16[192,768]{1,0:T(8,128)(2,1)S(1)} collective-permute-done((bf16[192,768]{1,0:T(8,128)(2,1)S(1)}, bf16[192,768]{1,0:T(8,128)(2,1)S(1)}, u32[]{:S(2)}, u32[]{:S(2)}) %collective-permute-start.5) | collective-permute-done | bytes 294944 | tf_op jit(solution)/shard_map/ppermute | solution.py:48
  22.4 1.2 %collective-permute-start.10 = (bf16[192,768]{1,0:T(8,128)(2,1)S(1)}, bf16[192,768]{1,0:T(8,128)(2,1)S(1)}, u32[]{:S(2)}, u32[]{:S(2)}) collective-permute-start(bf16[192,768]{1,0:T(8,128)(2,1)S(1)} %collective-permute-done.5.refs_2_), channel_id=1, source_target_pairs={{0,16},{16,0},{1,17},{17,1},{2,18},{18,2},{3,19},{19,3},{4,20},{20... | collective-permute-start | bytes 884744 | tf_op jit(solution)/shard_map/ppermute | solution.py:570
  23.7 0.1 collective-permute-start.6
  23.8 0.6 corners.1
  24.4 2.1 %collective-permute-done.6.refs_1_ = bf16[8,768]{1,0:T(8,128)(2,1)S(1)} collective-permute-done((bf16[8,768]{1,0:T(8,128)(2,1)S(1)}, bf16[8,768]{1,0:T(8,128)(2,1)S(1)}, u32[]{:S(2)}, u32[]{:S(2)}) %collective-permute-start.6) | collective-permute-done | bytes 12320 | tf_op jit(solution)/shard_map/ppermute | solution.py:48
  26.6 1.9 %collective-permute-start.8 = (bf16[4,8,768]{2,1,0:T(8,128)(2,1)S(1)}, bf16[4,8,768]{2,1,0:T(8,128)(2,1)S(1)}, u32[]{:S(2)}, u32[]{:S(2)}) collective-permute-start(bf16[4,8,768]{2,1,0:T(8,128)(2,1)S(1)} %get-tuple-element.47), channel_id=1, source_target_pairs={{1,2},{2,1},{5,6},{6,5},{9,10},{10,9},{13,14},{14,13},{17,18},{18,... | collective-permute-start | bytes 147464 | tf_op jit(solution)/shard_map/ppermute | solution.py:42
  28.5 2.9 %collective-permute-done.8.refs_5_ = bf16[4,8,768]{2,1,0:T(8,128)(2,1)S(1)} collective-permute-done((bf16[4,8,768]{2,1,0:T(8,128)(2,1)S(1)}, bf16[4,8,768]{2,1,0:T(8,128)(2,1)S(1)}, u32[]{:S(2)}, u32[]{:S(2)}) %collective-permute-start.8) | collective-permute-done | bytes 49184 | tf_op jit(solution)/shard_map/ppermute | solution.py:42
  31.4 2.1 %halo_norm.1 = (bf16[1600,768]{1,0:T(8,128)(2,1)S(1)}, f32[16,8,256]{2,1,0:T(8,128)S(1)}) custom-call(s32[10]{0:T(128)S(1)} %stack.63.place_ref, bf16[1024,768]{1,0:T(8,128)(2,1)S(1)} %own_norm.1.xq_ref.refs_8_, bf16[32,32,128]{2,1,0:T(8,128)(2,1)S(1)} %get-tuple-element.43.mark_ref, bf16[4,32,768]{2,1,0:T(8,128)(2,1)S(1)} %collective-permute-done.2.even_rows_ref.refs_0_, ...), custom_call_target="tpu_custom_call" | custom-call | flops 10000000 | bytes 6000000 | tf_op jit(solution)/shard_map/halo_norm/pallas_call | solution.py:591
  33.6 4.6 %collective-permute-start.9 = (bf16[192,768]{1,0:T(8,128)(2,1)S(1)}, bf16[192,768]{1,0:T(8,128)(2,1)S(1)}, u32[]{:S(2)}, u32[]{:S(2)}) collective-permute-start(bf16[192,768]{1,0:T(8,128)(2,1)S(1)} %collective-permute-done.5.refs_2_), channel_id=1, source_target_pairs={{0,4},{4,0},{8,12},{12,8},{1,5},{5,1},{9,13},{13,9},{2,6},{6,2},{1... | collective-permute-start | bytes 884744 | tf_op jit(solution)/shard_map/ppermute | solution.py:48
  38.2 0.1 collective-permute-start.13
  38.3 0.4 collective-permute-start.11
  38.8 0.6 collective-permute-done.9.refs_3_
  39.4 0.4 collective-permute-start.14
  39.8 0.4 collective-permute-done.11.refs_5_
  40.2 8.2 %project.1 = (bf16[3,1024,256]{2,1,0:T(8,128)(2,1)S(1)}, bf16[3,1600,256]{2,1,0:T(8,128)(2,1)S(1)}, bf16[3,1600,256]{2,1,0:T(8,128)(2,1)S(1)}, bf16[2304,768]{1,0:T(8,128)(2,1)S(1)}) custom-call(s32[10]{0:T(128)S(1)} %stack.63.place_ref, bf16[576,768]{1,0:T(8,128)(2,1)S(1)} %bitcast.13, bf16[576,768]{1,0:T(8,128)(2,1)S(1)} %collective-permute-done.4.refs_1_, ...), custom_call_target="tpu_custom_call" | custom-call | flops 5000000000 | bytes 14000000 | tf_op jit(solution)/shard_map/project/pallas_call | solution.py:620
  48.4 0.5 collective-permute-start.16
  48.9 1.2 %collective-permute-done.16.refs_3_ = bf16[208,768]{1,0:T(8,128)(2,1)S(1)} collective-permute-done((bf16[208,768]{1,0:T(8,128)(2,1)S(1)}, bf16[208,768]{1,0:T(8,128)(2,1)S(1)}, u32[]{:S(2)}, u32[]{:S(2)}) %collective-permute-start.16) | collective-permute-done | bytes 319520 | tf_op jit(solution)/shard_map/ppermute | solution.py:48
  50.1 3.9 %carriers.1 = (bf16[2,2,768]{2,1,0:T(2,128)(2,1)}, bf16[768,768]{1,0:T(8,128)(2,1)S(1)}, bf16[12,256,256]{2,1,0:T(8,128)(2,1)S(1)}, f32[8,768]{1,0:T(8,128)S(1)}) custom-call(s32[10]{0:T(128)S(1)} %stack.63.place_ref, bf16[2304,768]{1,0:T(8,128)(2,1)S(1)} %get-tuple-element.58.wt, bf16[208,768]{1,0:T(8,128)(2,1)S(1)} %final_pack.1.refs_0_, ...), custom_call_target="tpu_custom_call" | custom-call | flops 500000000 | bytes 5000000 | tf_op jit(solution)/shard_map/carriers/pallas_call | solution.py:641
  54.0 7.0 %attend.1.mix_s = bf16[1024,768]{1,0:T(8,128)(2,1)S(1)} custom-call(bf16[3,1024,256]{2,1,0:T(8,128)(2,1)S(1)} %get-tuple-element.54.q_s, bf16[3,1600,256]{2,1,0:T(8,128)(2,1)S(1)} %get-tuple-element.55.k_s, bf16[3,1600,256]{2,1,0:T(8,128)(2,1)S(1)} %get-tuple-element.56.v_s, f32[16,8,256]{2,1,0:T(8,128)S(1)} %get-tuple-element.57.hide_ref, ...), custom_call_target="tpu_custom_call" | custom-call | flops 4000000000 | bytes 12000000 | tf_op jit(solution)/shard_map/attend/pallas_call | solution.py:661
  61.0 2.4 %out.1 = bf16[32,32,768]{2,1,0:T(8,128)(2,1)} custom-call(bf16[32,32,768]{2,1,0:T(8,128)(2,1)S(1)} %get-tuple-element.33.x_ref, bf16[1024,768]{1,0:T(8,128)(2,1)S(1)} %attend.1.mix_s, bf16[768,768]{1,0:T(8,128)(2,1)S(1)} %get-tuple-element.62.wo), custom_call_target="tpu_custom_call" | custom-call | flops 1200000000 | bytes 6000000 | tf_op jit(solution)/shard_map/out/pallas_call | solution.py:676
  (22 shorter events, 0.3 us)
Async XLA Ops:
  0.8 0.7 %copy-start.2 = (bf16[2,2,768]{2,1,0:T(2,128)(2,1)S(1)}, bf16[2,2,768]{2,1,0:T(2,128)(2,1)}, u32[]{:S(2)}) copy-start(bf16[2,2,768]{2,1,0:T(2,128)(2,1)} %own_ref.1) | copy-start | bytes 18436
  3.7 12.6 %collective-permute-start = (bf16[17,8,768]{2,1,0:T(8,128)(2,1)S(1)}, bf16[17,8,768]{2,1,0:T(8,128)(2,1)S(1)}, u32[]{:S(2)}, u32[]{:S(2)}) collective-permute-start(bf16[17,8,768]{2,1,0:T(8,128)(2,1)S(1)} %get-tuple-element.34), channel_id=1, source_target_pairs={{0,1},{2,3},{1,0},{3,2},{4,5},{6,7},{5,4},{7,6},{8,9},{10,11},{9,8... | collective-permute-start | bytes 626696 | tf_op jit(solution)/shard_map/ppermute | solution.py:42
  3.8 12.5 %collective-permute-start.1 = (bf16[16,8,768]{2,1,0:T(8,128)(2,1)S(1)}, bf16[16,8,768]{2,1,0:T(8,128)(2,1)S(1)}, u32[]{:S(2)}, u32[]{:S(2)}) collective-permute-start(bf16[16,8,768]{2,1,0:T(8,128)(2,1)S(1)} %get-tuple-element.35), channel_id=1, source_target_pairs={{1,2},{2,1},{5,6},{6,5},{9,10},{10,9},{13,14},{14,13},{17,18},{18,... | collective-permute-start | bytes 589832 | tf_op jit(solution)/shard_map/ppermute | solution.py:42
  8.3 8.0 %collective-permute-start.3 = (bf16[4,32,768]{2,1,0:T(8,128)(2,1)S(1)}, bf16[4,32,768]{2,1,0:T(8,128)(2,1)S(1)}, u32[]{:S(2)}, u32[]{:S(2)}) collective-permute-start(bf16[4,32,768]{2,1,0:T(8,128)(2,1)S(1)} %get-tuple-element.37), channel_id=1, source_target_pairs={{4,8},{8,4},{5,9},{9,5},{6,10},{10,6},{7,11},{11,7},{20,24},{24,20... | collective-permute-start | bytes 589832 | tf_op jit(solution)/shard_map/ppermute | solution.py:42
  12.6 3.7 %collective-permute-start.2 = (bf16[4,32,768]{2,1,0:T(8,128)(2,1)S(1)}, bf16[4,32,768]{2,1,0:T(8,128)(2,1)S(1)}, u32[]{:S(2)}, u32[]{:S(2)}) collective-permute-start(bf16[4,32,768]{2,1,0:T(8,128)(2,1)S(1)} %get-tuple-element.36), channel_id=1, source_target_pairs={{0,4},{8,12},{4,0},{12,8},{1,5},{9,13},{5,1},{13,9},{2,6},{10,14},... | collective-permute-start | bytes 589832 | tf_op jit(solution)/shard_map/ppermute | solution.py:42
  14.3 8.1 %collective-permute-start.5 = (bf16[192,768]{1,0:T(8,128)(2,1)S(1)}, bf16[192,768]{1,0:T(8,128)(2,1)S(1)}, u32[]{:S(2)}, u32[]{:S(2)}) collective-permute-start(bf16[192,768]{1,0:T(8,128)(2,1)S(1)} %get-tuple-element.40), channel_id=1, source_target_pairs={{0,8},{4,12},{8,0},{12,4},{1,9},{5,13},{9,1},{13,5},{2,10},{6,14},... | collective-permute-start | bytes 884744 | tf_op jit(solution)/shard_map/ppermute | solution.py:48
  14.4 1.9 %copy-start = (bf16[768,576]{0,1:T(8,128)(2,1)S(1)}, bf16[768,576]{0,1:T(8,128)(2,1)}, u32[]{:S(2)}) copy-start(bf16[768,576]{0,1:T(8,128)(2,1)} %param.7) | copy-start | bytes 2654212
  14.4 9.2 %copy-start.3 = (bf16[2,2,768]{2,1,0:T(2,128)(2,1)S(1)}, bf16[2,2,768]{2,1,0:T(2,128)(2,1)}, u32[]{:S(2)}) copy-start(bf16[2,2,768]{2,1,0:T(2,128)(2,1)} %own_ref.1) | copy-start | bytes 18436
  16.3 23.9 %collective-permute-start.4 = (bf16[576,768]{1,0:T(8,128)(2,1)S(1)}, bf16[576,768]{1,0:T(8,128)(2,1)S(1)}, u32[]{:S(2)}, u32[]{:S(2)}) collective-permute-start(bf16[576,768]{1,0:T(8,128)(2,1)S(1)} %bitcast.12), channel_id=1, source_target_pairs={{0,4},{4,0},{8,12},{12,8},{1,5},{5,1},{9,13},{13,9},{2,6},{6,2},{1... | collective-permute-start | bytes 2654216 | tf_op jit(solution)/shard_map/ppermute | solution.py:48
  16.8 21.4 %collective-permute-start.12 = (bf16[192,768]{1,0:T(8,128)(2,1)S(1)}, bf16[192,768]{1,0:T(8,128)(2,1)S(1)}, u32[]{:S(2)}, u32[]{:S(2)}) collective-permute-start(bf16[192,768]{1,0:T(8,128)(2,1)S(1)} %get-tuple-element.52), channel_id=1, source_target_pairs={{0,8},{4,12},{8,0},{12,4},{1,9},{5,13},{9,1},{13,5},{2,10},{6,14},... | collective-permute-start | bytes 884744 | tf_op jit(solution)/shard_map/ppermute | solution.py:48
  22.4 15.8 %collective-permute-start.10 = (bf16[192,768]{1,0:T(8,128)(2,1)S(1)}, bf16[192,768]{1,0:T(8,128)(2,1)S(1)}, u32[]{:S(2)}, u32[]{:S(2)}) collective-permute-start(bf16[192,768]{1,0:T(8,128)(2,1)S(1)} %collective-permute-done.5.refs_2_), channel_id=1, source_target_pairs={{0,16},{16,0},{1,17},{17,1},{2,18},{18,2},{3,19},{19,3},{4,20},{20... | collective-permute-start | bytes 884744 | tf_op jit(solution)/shard_map/ppermute | solution.py:570
  23.7 15.0 %copy-start.1 = (bf16[768,192]{0,1:T(8,128)(2,1)S(1)}, bf16[768,192]{0,1:T(8,128)(2,1)}, u32[]{:S(2)}) copy-start(bf16[768,192]{0,1:T(8,128)(2,1)} %param.8) | copy-start | bytes 884740
  23.7 2.9 %collective-permute-start.6 = (bf16[8,768]{1,0:T(8,128)(2,1)S(1)}, bf16[8,768]{1,0:T(8,128)(2,1)S(1)}, u32[]{:S(2)}, u32[]{:S(2)}) collective-permute-start(bf16[8,768]{1,0:T(8,128)(2,1)S(1)} %carrier_pair.1.refs_0_), channel_id=1, source_target_pairs={{0,3},{1,2},{2,1},{3,0},{4,7},{5,6},{6,5},{7,4},{8,11},{9,10},{10,... | collective-permute-start | bytes 36872 | tf_op jit(solution)/shard_map/ppermute | solution.py:48
  24.4 4.1 %collective-permute-start.7 = (bf16[4,8,768]{2,1,0:T(8,128)(2,1)S(1)}, bf16[4,8,768]{2,1,0:T(8,128)(2,1)S(1)}, u32[]{:S(2)}, u32[]{:S(2)}) collective-permute-start(bf16[4,8,768]{2,1,0:T(8,128)(2,1)S(1)} %get-tuple-element.46), channel_id=1, source_target_pairs={{0,1},{2,3},{1,0},{3,2},{4,5},{6,7},{5,4},{7,6},{8,9},{10,11},{9,8... | collective-permute-start | bytes 147464 | tf_op jit(solution)/shard_map/ppermute | solution.py:42
  26.6 4.9 %collective-permute-start.8 = (bf16[4,8,768]{2,1,0:T(8,128)(2,1)S(1)}, bf16[4,8,768]{2,1,0:T(8,128)(2,1)S(1)}, u32[]{:S(2)}, u32[]{:S(2)}) collective-permute-start(bf16[4,8,768]{2,1,0:T(8,128)(2,1)S(1)} %get-tuple-element.47), channel_id=1, source_target_pairs={{1,2},{2,1},{5,6},{6,5},{9,10},{10,9},{13,14},{14,13},{17,18},{18,... | collective-permute-start | bytes 147464 | tf_op jit(solution)/shard_map/ppermute | solution.py:42
  33.6 5.8 %collective-permute-start.9 = (bf16[192,768]{1,0:T(8,128)(2,1)S(1)}, bf16[192,768]{1,0:T(8,128)(2,1)S(1)}, u32[]{:S(2)}, u32[]{:S(2)}) collective-permute-start(bf16[192,768]{1,0:T(8,128)(2,1)S(1)} %collective-permute-done.5.refs_2_), channel_id=1, source_target_pairs={{0,4},{4,0},{8,12},{12,8},{1,5},{5,1},{9,13},{13,9},{2,6},{6,2},{1... | collective-permute-start | bytes 884744 | tf_op jit(solution)/shard_map/ppermute | solution.py:48
  38.2 1.6 %collective-permute-start.13 = (bf16[192,768]{1,0:T(8,128)(2,1)S(1)}, bf16[192,768]{1,0:T(8,128)(2,1)S(1)}, u32[]{:S(2)}, u32[]{:S(2)}) collective-permute-start(bf16[192,768]{1,0:T(8,128)(2,1)S(1)} %collective-permute-done.12.refs_6_), channel_id=1, source_target_pairs={{0,4},{4,0},{8,12},{12,8},{1,5},{5,1},{9,13},{13,9},{2,6},{6,2},{1... | collective-permute-start | bytes 884744 | tf_op jit(solution)/shard_map/ppermute | solution.py:48
  38.3 2.0 %collective-permute-start.11 = (bf16[192,768]{1,0:T(8,128)(2,1)S(1)}, bf16[192,768]{1,0:T(8,128)(2,1)S(1)}, u32[]{:S(2)}, u32[]{:S(2)}) collective-permute-start(bf16[192,768]{1,0:T(8,128)(2,1)S(1)} %collective-permute-done.10.refs_4_), channel_id=1, source_target_pairs={{0,4},{4,0},{8,12},{12,8},{1,5},{5,1},{9,13},{13,9},{2,6},{6,2},{1... | collective-permute-start | bytes 884744 | tf_op jit(solution)/shard_map/ppermute | solution.py:48
  38.7 9.7 %collective-permute-start.15 = (bf16[208,768]{1,0:T(8,128)(2,1)S(1)}, bf16[208,768]{1,0:T(8,128)(2,1)S(1)}, u32[]{:S(2)}, u32[]{:S(2)}) collective-permute-start(bf16[208,768]{1,0:T(8,128)(2,1)S(1)} %final_pack.1.refs_0_), channel_id=1, source_target_pairs={{0,8},{4,12},{8,0},{12,4},{1,9},{5,13},{9,1},{13,5},{2,10},{6,14},... | collective-permute-start | bytes 958472 | tf_op jit(solution)/shard_map/ppermute | solution.py:48
  39.4 9.5 %collective-permute-start.14 = (bf16[208,768]{1,0:T(8,128)(2,1)S(1)}, bf16[208,768]{1,0:T(8,128)(2,1)S(1)}, u32[]{:S(2)}, u32[]{:S(2)}) collective-permute-start(bf16[208,768]{1,0:T(8,128)(2,1)S(1)} %final_pack.1.refs_0_), channel_id=1, source_target_pairs={{0,4},{4,0},{8,12},{12,8},{1,5},{5,1},{9,13},{13,9},{2,6},{6,2},{1... | collective-permute-start | bytes 958472 | tf_op jit(solution)/shard_map/ppermute | solution.py:48
  48.4 1.7 %collective-permute-start.16 = (bf16[208,768]{1,0:T(8,128)(2,1)S(1)}, bf16[208,768]{1,0:T(8,128)(2,1)S(1)}, u32[]{:S(2)}, u32[]{:S(2)}) collective-permute-start(bf16[208,768]{1,0:T(8,128)(2,1)S(1)} %collective-permute-done.15.refs_2_), channel_id=1, source_target_pairs={{0,4},{4,0},{8,12},{12,8},{1,5},{5,1},{9,13},{13,9},{2,6},{6,2},{1... | collective-permute-start | bytes 958472 | tf_op jit(solution)/shard_map/ppermute | solution.py:48

commit v2 on v1

--- a/solution.py
+++ b/solution.py
@@ -483,6 +483,21 @@
     place = [row_at == 0, row_at == row - 1, col_at == 0, col_at == col - 1, row_at % 2 == 0, col_at % 2 == 0, row_at]
     place = jnp.stack([jnp.asarray(p).astype(jnp.int32) for p in place + [start * piece_rows for start in starts]])
 
+    mine, last = pl.pallas_call(
+        piece_kernel,
+        out_shape=(
+            pltpu.VMEM((piece_rows, channels), jnp.bfloat16),
+            pltpu.VMEM((triple_t.shape[0] - relays * piece_rows, channels), jnp.bfloat16),
+        ),
+        in_specs=[scalars, hbm],
+        out_specs=(vmem, vmem),
+        scratch_shapes=[pltpu.SemaphoreType.DMA((2,))],
+        compiler_params=small,
+        cost_estimate=pl.CostEstimate(flops=1_000_000, bytes_accessed=1_000_000, transcendentals=0),
+        name="pieces",
+    )(place, pltpu.with_memory_space_constraint(triple_t, pltpu.HBM))
+    place = after(place, mine)
+
     mark, even_rows, odd_rows, even_cols, odd_cols, x = pl.pallas_call(
         edge_kernel,
         out_shape=(
@@ -505,19 +520,6 @@
         cost_estimate=pl.CostEstimate(flops=1_000_000, bytes_accessed=1_000_000, transcendentals=0),
         name="edge_rows",
     )(place, *(pltpu.with_memory_space_constraint(a, pltpu.HBM) for a in (genuine_flags, grid_elements)), summary_vectors)
-    mine, last = pl.pallas_call(
-        piece_kernel,
-        out_shape=(
-            pltpu.VMEM((piece_rows, channels), jnp.bfloat16),
-            pltpu.VMEM((triple_t.shape[0] - relays * piece_rows, channels), jnp.bfloat16),
-        ),
-        in_specs=[scalars, hbm],
-        out_specs=(vmem, vmem),
-        scratch_shapes=[pltpu.SemaphoreType.DMA((2,))],
-        compiler_params=small,
-        cost_estimate=pl.CostEstimate(flops=1_000_000, bytes_accessed=1_000_000, transcendentals=0),
-        name="pieces",
-    )(place, pltpu.with_memory_space_constraint(after(triple_t, even_rows), pltpu.HBM))
     xq = pl.pallas_call(
         own_kernel,
         out_shape=pltpu.VMEM((rows * cols, channels), jnp.bfloat16),
@@ -566,7 +568,6 @@
         got = swapped(carriers, "col", 2 * bit - 1)
         parts.append(got)
     if relays:
-        first = after(first, even_cols, odd_cols)
         others = [lax.ppermute(first, "img", [(i, (i + k) % img) for i in range(img)]) for k in range(1, relays)]
         far_pieces = [first] + others
     far_pieces.append(far_last)
@@ -580,7 +581,7 @@
         cost_estimate=pl.CostEstimate(flops=1_000, bytes_accessed=1_000, transcendentals=0),
         name="final_pack",
     )(final_t, *parts)
-    finals, triples, offsets = [final_pack], [after(triple_t, even_cols, odd_cols, even_rows, odd_rows, xq)], [0]
+    finals, triples, offsets = [final_pack], [after(triple_t, even_cols, odd_cols, even_rows, odd_rows, xq, first)], [0]
     for bit in rest:
         finals = finals + [swapped(p, "row", bit) for p in finals]
         triples = triples + [swapped(p, "row", bit) for p in triples]

time: 63.7 us -> 59.4 us (0.932)
  waiting for transfers between devices: 11.3 us -> 8.76 us
  starting transfers between devices: 20.5 us -> 18.8 us
    ppermute x10, waiting for transfers between devices: 8.33 us -> 4.3 us  [swapped(): return lax.ppermute(block, axis, [(i, i ^ bit) for i in range(count)])]
    ppermute x6, waiting for transfers between devices: 2.94 us -> 4.46 us  [pair_swapped(): got.append(lax.ppermute(block, axis, pairs + [(b, a) for a, b in pairs]))]
    ppermute x10, starting transfers between devices: 8.46 us -> 7.42 us  [swapped(): return lax.ppermute(block, axis, [(i, i ^ bit) for i in range(count)])]
    ppermute x6, starting transfers between devices: 10.9 us -> 10.1 us  [pair_swapped(): got.append(lax.ppermute(block, axis, pairs + [(b, a) for a, b in pairs]))]
  transfers between devices with their start and end apart: 17 -> 17, of which waited for: 6 -> 6; matrix products, arithmetic and copies ran while one was open for 0% -> 0% of each run, Pallas kernels for 23% -> 25%
where the time goes in v2:
time: 59.4 us; the launch traced here: 59.1 us
  Pallas kernels  29.9 us (50%)
  starting transfers between devices  18.8 us (32%)
  waiting for transfers between devices  8.76 us (15%)
  between operations  0.87 us (1%)
  local copies, waits for them, and re-layouts  0.79 us (1%)
    ppermute x6, starting transfers between devices, pair_swapped(): got.append(lax.ppermute(block, axis, pairs + [(b, a) for a, b in pairs]))  10.1 us
    pallas_call x1, Pallas kernels, local(): pl.pallas_call(functools.partial(project_kernel, offsets, numbered, tripl...  8.2 us
    ppermute x10, starting transfers between devices, swapped(): return lax.ppermute(block, axis, [(i, i ^ bit) for i in range(count)])  7.42 us
    pallas_call x1, Pallas kernels, local(): pl.pallas_call(functools.partial(attend_kernel, rows // TILE, cols // TIL...  6.98 us
    ppermute x6, waiting for transfers between devices, pair_swapped(): got.append(lax.ppermute(block, axis, pairs + [(b, a) for a, b in pairs]))  4.46 us
    ppermute x10, waiting for transfers between devices, swapped(): return lax.ppermute(block, axis, [(i, i ^ bit) for i in range(count)])  4.3 us
    pallas_call x1, Pallas kernels, local(): pl.pallas_call(functools.partial(carrier_kernel, offsets), out_shape=(jax...  3.86 us
    pallas_call x1, Pallas kernels, local(): pl.pallas_call(out_kernel, out_shape=jax.ShapeDtypeStruct(grid_elements.s...  2.35 us
  transfers between devices with their start and end apart: 17, of which 6 were waited for; matrix products, arithmetic and copies ran while one was open for 0% of the time, Pallas kernels for 25%

profile of v2, /device:TPU:9, one launch (start us, length us, event | category | flops | bytes accessed | tf_op | source)
XLA Modules:
  0.0 59.1 jit_solution(9024825124007518832)
XLA Ops:
  0.7 0.1 stack.63.place_ref
  0.8 1.6 %pieces.1 = (bf16[192,768]{1,0:T(8,128)(2,1)S(1)}, bf16[192,768]{1,0:T(8,128)(2,1)S(1)}) custom-call(s32[10]{0:T(128)S(1)} %stack.63.place_ref, bf16[576,768]{1,0:T(8,128)(2,1)} %bitcast.11), custom_call_target="tpu_custom_call" | custom-call | flops 1000000 | bytes 1000000 | tf_op jit(solution)/shard_map/pieces/pallas_call | solution.py:486
  2.4 1.3 %collective-permute-start.4 = (bf16[192,768]{1,0:T(8,128)(2,1)S(1)}, bf16[192,768]{1,0:T(8,128)(2,1)S(1)}, u32[]{:S(2)}, u32[]{:S(2)}) collective-permute-start(bf16[192,768]{1,0:T(8,128)(2,1)S(1)} %get-tuple-element.32), channel_id=1, source_target_pairs={{0,8},{4,12},{8,0},{12,4},{1,9},{5,13},{9,1},{13,5},{2,10},{6,14},... | collective-permute-start | bytes 884744 | tf_op jit(solution)/shard_map/ppermute | solution.py:48
  3.7 0.7 %copy-done.2 = bf16[2,2,768]{2,1,0:T(2,128)(2,1)S(1)} copy-done((bf16[2,2,768]{2,1,0:T(2,128)(2,1)S(1)}, bf16[2,2,768]{2,1,0:T(2,128)(2,1)}, u32[]{:S(2)}) %copy-start.2) | copy-done | bytes 6168
  4.4 2.3 %edge_rows.1 = (bf16[32,32,128]{2,1,0:T(8,128)(2,1)S(1)}, bf16[4,32,768]{2,1,0:T(8,128)(2,1)S(1)}, bf16[4,32,768]{2,1,0:T(8,128)(2,1)S(1)}, bf16[17,8,768]{2,1,0...) custom-call(s32[10]{0:T(128)S(1)} %stack.63.place_ref, s32[32,32]{1,0:T(8,128)} %flags_hbm.1, ...), custom_call_target="tpu_custom_call" | custom-call | flops 1000000 | bytes 1000000 | tf_op jit(solution)/shard_map/edge_rows/pallas_call | solution.py:501
  6.7 0.2 collective-permute-start
  6.9 4.3 %collective-permute-start.1 = (bf16[16,8,768]{2,1,0:T(8,128)(2,1)S(1)}, bf16[16,8,768]{2,1,0:T(8,128)(2,1)S(1)}, u32[]{:S(2)}, u32[]{:S(2)}) collective-permute-start(bf16[16,8,768]{2,1,0:T(8,128)(2,1)S(1)} %get-tuple-element.36), channel_id=1, source_target_pairs={{1,2},{2,1},{5,6},{6,5},{9,10},{10,9},{13,14},{14,13},{17,18},{18,... | collective-permute-start | bytes 589832 | tf_op jit(solution)/shard_map/ppermute | solution.py:42
  11.2 3.5 %collective-permute-start.3 = (bf16[4,32,768]{2,1,0:T(8,128)(2,1)S(1)}, bf16[4,32,768]{2,1,0:T(8,128)(2,1)S(1)}, u32[]{:S(2)}, u32[]{:S(2)}) collective-permute-start(bf16[4,32,768]{2,1,0:T(8,128)(2,1)S(1)} %get-tuple-element.38), channel_id=1, source_target_pairs={{4,8},{8,4},{5,9},{9,5},{6,10},{10,6},{7,11},{11,7},{20,24},{24,20... | collective-permute-start | bytes 589832 | tf_op jit(solution)/shard_map/ppermute | solution.py:42
  14.8 0.1 collective-permute-start.2
  14.9 1.8 %own_norm.1.xq_ref.refs_8_ = bf16[1024,768]{1,0:T(8,128)(2,1)S(1)} custom-call(bf16[32,32,768]{2,1,0:T(8,128)(2,1)S(1)} %get-tuple-element.34.x_ref), custom_call_target="tpu_custom_call" | custom-call | flops 1000000 | bytes 1000000 | tf_op jit(solution)/shard_map/own_norm/pallas_call | solution.py:523
  16.7 1.5 %collective-permute-done.3.odd_rows_ref.refs_1_ = bf16[4,32,768]{2,1,0:T(8,128)(2,1)S(1)} collective-permute-done((bf16[4,32,768]{2,1,0:T(8,128)(2,1)S(1)}, bf16[4,32,768]{2,1,0:T(8,128)(2,1)S(1)}, u32[]{:S(2)}, u32[]{:S(2)}) %collective-permute-start.3) | collective-permute-done | bytes 196640 | tf_op jit(solution)/shard_map/ppermute | solution.py:42
  18.2 0.1 collective-permute-start.5
  18.3 1.7 %collective-permute-start.12 = (bf16[192,768]{1,0:T(8,128)(2,1)S(1)}, bf16[192,768]{1,0:T(8,128)(2,1)S(1)}, u32[]{:S(2)}, u32[]{:S(2)}) collective-permute-start(bf16[192,768]{1,0:T(8,128)(2,1)S(1)} %get-tuple-element.50), channel_id=1, source_target_pairs={{0,8},{4,12},{8,0},{12,4},{1,9},{5,13},{9,1},{13,5},{2,10},{6,14},... | collective-permute-start | bytes 884744 | tf_op jit(solution)/shard_map/ppermute | solution.py:48
  20.1 1.2 %collective-permute-start.10 = (bf16[192,768]{1,0:T(8,128)(2,1)S(1)}, bf16[192,768]{1,0:T(8,128)(2,1)S(1)}, u32[]{:S(2)}, u32[]{:S(2)}) collective-permute-start(bf16[192,768]{1,0:T(8,128)(2,1)S(1)} %collective-permute-done.4.refs_2_), channel_id=1, source_target_pairs={{0,16},{16,0},{1,17},{17,1},{2,18},{18,2},{3,19},{19,3},{4,20},{20... | collective-permute-start | bytes 884744 | tf_op jit(solution)/shard_map/ppermute | solution.py:571
  21.4 0.6 %corners.1 = (bf16[4,8,768]{2,1,0:T(8,128)(2,1)S(1)}, bf16[4,8,768]{2,1,0:T(8,128)(2,1)S(1)}) custom-call(s32[10]{0:T(128)S(1)} %stack.63.place_ref, bf16[4,32,768]{2,1,0:T(8,128)(2,1)S(1)} %collective-permute-done.2.even_rows_ref.refs_0_, bf16[4,32,768]{2,1,0:T(8,128)(2,1)S(1)} %collective-permute-done.3.odd_rows_ref.refs_1_), custom_call_target="tpu_custom_call" | custom-call | flops 1000000 | bytes 1000000 | tf_op jit(solution)/shard_map/corners/pallas_call | solution.py:540
  22.1 2.1 %collective-permute-done.6.refs_1_ = bf16[8,768]{1,0:T(8,128)(2,1)S(1)} collective-permute-done((bf16[8,768]{1,0:T(8,128)(2,1)S(1)}, bf16[8,768]{1,0:T(8,128)(2,1)S(1)}, u32[]{:S(2)}, u32[]{:S(2)}) %collective-permute-start.6) | collective-permute-done | bytes 12320 | tf_op jit(solution)/shard_map/ppermute | solution.py:48
  24.2 1.9 %collective-permute-start.8 = (bf16[4,8,768]{2,1,0:T(8,128)(2,1)S(1)}, bf16[4,8,768]{2,1,0:T(8,128)(2,1)S(1)}, u32[]{:S(2)}, u32[]{:S(2)}) collective-permute-start(bf16[4,8,768]{2,1,0:T(8,128)(2,1)S(1)} %get-tuple-element.45), channel_id=1, source_target_pairs={{1,2},{2,1},{5,6},{6,5},{9,10},{10,9},{13,14},{14,13},{17,18},{18,... | collective-permute-start | bytes 147464 | tf_op jit(solution)/shard_map/ppermute | solution.py:42
  26.1 2.9 %collective-permute-done.8.refs_5_ = bf16[4,8,768]{2,1,0:T(8,128)(2,1)S(1)} collective-permute-done((bf16[4,8,768]{2,1,0:T(8,128)(2,1)S(1)}, bf16[4,8,768]{2,1,0:T(8,128)(2,1)S(1)}, u32[]{:S(2)}, u32[]{:S(2)}) %collective-permute-start.8) | collective-permute-done | bytes 49184 | tf_op jit(solution)/shard_map/ppermute | solution.py:42
  29.1 2.1 %halo_norm.1 = (bf16[1600,768]{1,0:T(8,128)(2,1)S(1)}, f32[16,8,256]{2,1,0:T(8,128)S(1)}) custom-call(s32[10]{0:T(128)S(1)} %stack.63.place_ref, bf16[1024,768]{1,0:T(8,128)(2,1)S(1)} %own_norm.1.xq_ref.refs_8_, bf16[32,32,128]{2,1,0:T(8,128)(2,1)S(1)} %get-tuple-element.41.mark_ref, bf16[4,32,768]{2,1,0:T(8,128)(2,1)S(1)} %collective-permute-done.2.even_rows_ref.refs_0_, ...), custom_call_target="tpu_custom_call" | custom-call | flops 10000000 | bytes 6000000 | tf_op jit(solution)/shard_map/halo_norm/pallas_call | solution.py:592
  31.2 2.6 %collective-permute-start.9 = (bf16[192,768]{1,0:T(8,128)(2,1)S(1)}, bf16[192,768]{1,0:T(8,128)(2,1)S(1)}, u32[]{:S(2)}, u32[]{:S(2)}) collective-permute-start(bf16[192,768]{1,0:T(8,128)(2,1)S(1)} %collective-permute-done.4.refs_2_), channel_id=1, source_target_pairs={{0,4},{4,0},{8,12},{12,8},{1,5},{5,1},{9,13},{13,9},{2,6},{6,2},{1... | collective-permute-start | bytes 884744 | tf_op jit(solution)/shard_map/ppermute | solution.py:48
  33.9 0.1 collective-permute-start.13
  34.0 0.4 collective-permute-start.11
  34.4 0.2 collective-permute-start.15
  34.6 0.4 collective-permute-done.9.refs_3_
  35.1 0.4 collective-permute-start.14
  35.5 0.4 collective-permute-done.11.refs_5_
  35.9 8.2 %project.1 = (bf16[3,1024,256]{2,1,0:T(8,128)(2,1)S(1)}, bf16[3,1600,256]{2,1,0:T(8,128)(2,1)S(1)}, bf16[3,1600,256]{2,1,0:T(8,128)(2,1)S(1)}, bf16[2304,768]{1,0:T(8,128)(2,1)S(1)}) custom-call(s32[10]{0:T(128)S(1)} %stack.63.place_ref, bf16[576,768]{1,0:T(8,128)(2,1)S(1)} %bitcast.13, bf16[576,768]{1,0:T(8,128)(2,1)S(1)} %collective-permute-done.5.refs_1_, ...), custom_call_target="tpu_custom_call" | custom-call | flops 5000000000 | bytes 14000000 | tf_op jit(solution)/shard_map/project/pallas_call | solution.py:621
  44.1 0.5 collective-permute-start.16
  44.6 1.2 %collective-permute-done.16.refs_3_ = bf16[208,768]{1,0:T(8,128)(2,1)S(1)} collective-permute-done((bf16[208,768]{1,0:T(8,128)(2,1)S(1)}, bf16[208,768]{1,0:T(8,128)(2,1)S(1)}, u32[]{:S(2)}, u32[]{:S(2)}) %collective-permute-start.16) | collective-permute-done | bytes 319520 | tf_op jit(solution)/shard_map/ppermute | solution.py:48
  45.8 3.9 %carriers.1 = (bf16[2,2,768]{2,1,0:T(2,128)(2,1)}, bf16[768,768]{1,0:T(8,128)(2,1)S(1)}, bf16[12,256,256]{2,1,0:T(8,128)(2,1)S(1)}, f32[8,768]{1,0:T(8,128)S(1)}) custom-call(s32[10]{0:T(128)S(1)} %stack.63.place_ref, bf16[2304,768]{1,0:T(8,128)(2,1)S(1)} %get-tuple-element.56.wt, bf16[208,768]{1,0:T(8,128)(2,1)S(1)} %final_pack.1.refs_0_, ...), custom_call_target="tpu_custom_call" | custom-call | flops 500000000 | bytes 5000000 | tf_op jit(solution)/shard_map/carriers/pallas_call | solution.py:642
  49.7 7.0 %attend.1.mix_s = bf16[1024,768]{1,0:T(8,128)(2,1)S(1)} custom-call(bf16[3,1024,256]{2,1,0:T(8,128)(2,1)S(1)} %get-tuple-element.52.q_s, bf16[3,1600,256]{2,1,0:T(8,128)(2,1)S(1)} %get-tuple-element.53.k_s, bf16[3,1600,256]{2,1,0:T(8,128)(2,1)S(1)} %get-tuple-element.54.v_s, f32[16,8,256]{2,1,0:T(8,128)S(1)} %get-tuple-element.55.hide_ref, ...), custom_call_target="tpu_custom_call" | custom-call | flops 4000000000 | bytes 12000000 | tf_op jit(solution)/shard_map/attend/pallas_call | solution.py:662
  56.7 2.4 %out.1 = bf16[32,32,768]{2,1,0:T(8,128)(2,1)} custom-call(bf16[32,32,768]{2,1,0:T(8,128)(2,1)S(1)} %get-tuple-element.34.x_ref, bf16[1024,768]{1,0:T(8,128)(2,1)S(1)} %attend.1.mix_s, bf16[768,768]{1,0:T(8,128)(2,1)S(1)} %get-tuple-element.60.wo), custom_call_target="tpu_custom_call" | custom-call | flops 1200000000 | bytes 6000000 | tf_op jit(solution)/shard_map/out/pallas_call | solution.py:677
  (20 shorter events, 0.3 us)
Async XLA Ops:
  2.4 15.8 %collective-permute-start.4 = (bf16[192,768]{1,0:T(8,128)(2,1)S(1)}, bf16[192,768]{1,0:T(8,128)(2,1)S(1)}, u32[]{:S(2)}, u32[]{:S(2)}) collective-permute-start(bf16[192,768]{1,0:T(8,128)(2,1)S(1)} %get-tuple-element.32), channel_id=1, source_target_pairs={{0,8},{4,12},{8,0},{12,4},{1,9},{5,13},{9,1},{13,5},{2,10},{6,14},... | collective-permute-start | bytes 884744 | tf_op jit(solution)/shard_map/ppermute | solution.py:48
  3.7 0.7 %copy-start.2 = (bf16[2,2,768]{2,1,0:T(2,128)(2,1)S(1)}, bf16[2,2,768]{2,1,0:T(2,128)(2,1)}, u32[]{:S(2)}) copy-start(bf16[2,2,768]{2,1,0:T(2,128)(2,1)} %own_ref.1) | copy-start | bytes 18436
  6.7 11.6 %collective-permute-start = (bf16[17,8,768]{2,1,0:T(8,128)(2,1)S(1)}, bf16[17,8,768]{2,1,0:T(8,128)(2,1)S(1)}, u32[]{:S(2)}, u32[]{:S(2)}) collective-permute-start(bf16[17,8,768]{2,1,0:T(8,128)(2,1)S(1)} %get-tuple-element.35), channel_id=1, source_target_pairs={{0,1},{2,3},{1,0},{3,2},{4,5},{6,7},{5,4},{7,6},{8,9},{10,11},{9,8... | collective-permute-start | bytes 626696 | tf_op jit(solution)/shard_map/ppermute | solution.py:42
  6.9 9.8 %collective-permute-start.1 = (bf16[16,8,768]{2,1,0:T(8,128)(2,1)S(1)}, bf16[16,8,768]{2,1,0:T(8,128)(2,1)S(1)}, u32[]{:S(2)}, u32[]{:S(2)}) collective-permute-start(bf16[16,8,768]{2,1,0:T(8,128)(2,1)S(1)} %get-tuple-element.36), channel_id=1, source_target_pairs={{1,2},{2,1},{5,6},{6,5},{9,10},{10,9},{13,14},{14,13},{17,18},{18,... | collective-permute-start | bytes 589832 | tf_op jit(solution)/shard_map/ppermute | solution.py:42
  11.2 7.0 %collective-permute-start.3 = (bf16[4,32,768]{2,1,0:T(8,128)(2,1)S(1)}, bf16[4,32,768]{2,1,0:T(8,128)(2,1)S(1)}, u32[]{:S(2)}, u32[]{:S(2)}) collective-permute-start(bf16[4,32,768]{2,1,0:T(8,128)(2,1)S(1)} %get-tuple-element.38), channel_id=1, source_target_pairs={{4,8},{8,4},{5,9},{9,5},{6,10},{10,6},{7,11},{11,7},{20,24},{24,20... | collective-permute-start | bytes 589832 | tf_op jit(solution)/shard_map/ppermute | solution.py:42
  14.8 3.4 %collective-permute-start.2 = (bf16[4,32,768]{2,1,0:T(8,128)(2,1)S(1)}, bf16[4,32,768]{2,1,0:T(8,128)(2,1)S(1)}, u32[]{:S(2)}, u32[]{:S(2)}) collective-permute-start(bf16[4,32,768]{2,1,0:T(8,128)(2,1)S(1)} %get-tuple-element.37), channel_id=1, source_target_pairs={{0,4},{8,12},{4,0},{12,8},{1,5},{9,13},{5,1},{13,9},{2,6},{10,14},... | collective-permute-start | bytes 589832 | tf_op jit(solution)/shard_map/ppermute | solution.py:42
  14.8 3.4 %copy-start = (bf16[768,576]{0,1:T(8,128)(2,1)S(1)}, bf16[768,576]{0,1:T(8,128)(2,1)}, u32[]{:S(2)}) copy-start(bf16[768,576]{0,1:T(8,128)(2,1)} %param.7) | copy-start | bytes 2654212
  18.2 17.7 %collective-permute-start.5 = (bf16[576,768]{1,0:T(8,128)(2,1)S(1)}, bf16[576,768]{1,0:T(8,128)(2,1)S(1)}, u32[]{:S(2)}, u32[]{:S(2)}) collective-permute-start(bf16[576,768]{1,0:T(8,128)(2,1)S(1)} %bitcast.12), channel_id=1, source_target_pairs={{0,4},{4,0},{8,12},{12,8},{1,5},{5,1},{9,13},{13,9},{2,6},{6,2},{1... | collective-permute-start | bytes 2654216 | tf_op jit(solution)/shard_map/ppermute | solution.py:48
  18.3 15.6 %collective-permute-start.12 = (bf16[192,768]{1,0:T(8,128)(2,1)S(1)}, bf16[192,768]{1,0:T(8,128)(2,1)S(1)}, u32[]{:S(2)}, u32[]{:S(2)}) collective-permute-start(bf16[192,768]{1,0:T(8,128)(2,1)S(1)} %get-tuple-element.50), channel_id=1, source_target_pairs={{0,8},{4,12},{8,0},{12,4},{1,9},{5,13},{9,1},{13,5},{2,10},{6,14},... | collective-permute-start | bytes 884744 | tf_op jit(solution)/shard_map/ppermute | solution.py:48
  20.1 13.9 %collective-permute-start.10 = (bf16[192,768]{1,0:T(8,128)(2,1)S(1)}, bf16[192,768]{1,0:T(8,128)(2,1)S(1)}, u32[]{:S(2)}, u32[]{:S(2)}) collective-permute-start(bf16[192,768]{1,0:T(8,128)(2,1)S(1)} %collective-permute-done.4.refs_2_), channel_id=1, source_target_pairs={{0,16},{16,0},{1,17},{17,1},{2,18},{18,2},{3,19},{19,3},{4,20},{20... | collective-permute-start | bytes 884744 | tf_op jit(solution)/shard_map/ppermute | solution.py:571
  21.3 13.1 %copy-start.1 = (bf16[768,192]{0,1:T(8,128)(2,1)S(1)}, bf16[768,192]{0,1:T(8,128)(2,1)}, u32[]{:S(2)}) copy-start(bf16[768,192]{0,1:T(8,128)(2,1)} %param.8) | copy-start | bytes 884740
  21.3 2.9 %collective-permute-start.6 = (bf16[8,768]{1,0:T(8,128)(2,1)S(1)}, bf16[8,768]{1,0:T(8,128)(2,1)S(1)}, u32[]{:S(2)}, u32[]{:S(2)}) collective-permute-start(bf16[8,768]{1,0:T(8,128)(2,1)S(1)} %carrier_pair.1.refs_0_), channel_id=1, source_target_pairs={{0,3},{1,2},{2,1},{3,0},{4,7},{5,6},{6,5},{7,4},{8,11},{9,10},{10,... | collective-permute-start | bytes 36872 | tf_op jit(solution)/shard_map/ppermute | solution.py:48
  22.0 4.1 %collective-permute-start.7 = (bf16[4,8,768]{2,1,0:T(8,128)(2,1)S(1)}, bf16[4,8,768]{2,1,0:T(8,128)(2,1)S(1)}, u32[]{:S(2)}, u32[]{:S(2)}) collective-permute-start(bf16[4,8,768]{2,1,0:T(8,128)(2,1)S(1)} %get-tuple-element.44), channel_id=1, source_target_pairs={{0,1},{2,3},{1,0},{3,2},{4,5},{6,7},{5,4},{7,6},{8,9},{10,11},{9,8... | collective-permute-start | bytes 147464 | tf_op jit(solution)/shard_map/ppermute | solution.py:42
  24.2 4.9 %collective-permute-start.8 = (bf16[4,8,768]{2,1,0:T(8,128)(2,1)S(1)}, bf16[4,8,768]{2,1,0:T(8,128)(2,1)S(1)}, u32[]{:S(2)}, u32[]{:S(2)}) collective-permute-start(bf16[4,8,768]{2,1,0:T(8,128)(2,1)S(1)} %get-tuple-element.45), channel_id=1, source_target_pairs={{1,2},{2,1},{5,6},{6,5},{9,10},{10,9},{13,14},{14,13},{17,18},{18,... | collective-permute-start | bytes 147464 | tf_op jit(solution)/shard_map/ppermute | solution.py:42
  31.2 3.9 %collective-permute-start.9 = (bf16[192,768]{1,0:T(8,128)(2,1)S(1)}, bf16[192,768]{1,0:T(8,128)(2,1)S(1)}, u32[]{:S(2)}, u32[]{:S(2)}) collective-permute-start(bf16[192,768]{1,0:T(8,128)(2,1)S(1)} %collective-permute-done.4.refs_2_), channel_id=1, source_target_pairs={{0,4},{4,0},{8,12},{12,8},{1,5},{5,1},{9,13},{13,9},{2,6},{6,2},{1... | collective-permute-start | bytes 884744 | tf_op jit(solution)/shard_map/ppermute | solution.py:48
  33.9 1.6 %collective-permute-start.13 = (bf16[192,768]{1,0:T(8,128)(2,1)S(1)}, bf16[192,768]{1,0:T(8,128)(2,1)S(1)}, u32[]{:S(2)}, u32[]{:S(2)}) collective-permute-start(bf16[192,768]{1,0:T(8,128)(2,1)S(1)} %collective-permute-done.12.refs_6_), channel_id=1, source_target_pairs={{0,4},{4,0},{8,12},{12,8},{1,5},{5,1},{9,13},{13,9},{2,6},{6,2},{1... | collective-permute-start | bytes 884744 | tf_op jit(solution)/shard_map/ppermute | solution.py:48
  34.0 2.0 %collective-permute-start.11 = (bf16[192,768]{1,0:T(8,128)(2,1)S(1)}, bf16[192,768]{1,0:T(8,128)(2,1)S(1)}, u32[]{:S(2)}, u32[]{:S(2)}) collective-permute-start(bf16[192,768]{1,0:T(8,128)(2,1)S(1)} %collective-permute-done.10.refs_4_), channel_id=1, source_target_pairs={{0,4},{4,0},{8,12},{12,8},{1,5},{5,1},{9,13},{13,9},{2,6},{6,2},{1... | collective-permute-start | bytes 884744 | tf_op jit(solution)/shard_map/ppermute | solution.py:48
  34.4 9.7 %collective-permute-start.15 = (bf16[208,768]{1,0:T(8,128)(2,1)S(1)}, bf16[208,768]{1,0:T(8,128)(2,1)S(1)}, u32[]{:S(2)}, u32[]{:S(2)}) collective-permute-start(bf16[208,768]{1,0:T(8,128)(2,1)S(1)} %final_pack.1.refs_0_), channel_id=1, source_target_pairs={{0,8},{4,12},{8,0},{12,4},{1,9},{5,13},{9,1},{13,5},{2,10},{6,14},... | collective-permute-start | bytes 958472 | tf_op jit(solution)/shard_map/ppermute | solution.py:48
  35.1 9.5 %collective-permute-start.14 = (bf16[208,768]{1,0:T(8,128)(2,1)S(1)}, bf16[208,768]{1,0:T(8,128)(2,1)S(1)}, u32[]{:S(2)}, u32[]{:S(2)}) collective-permute-start(bf16[208,768]{1,0:T(8,128)(2,1)S(1)} %final_pack.1.refs_0_), channel_id=1, source_target_pairs={{0,4},{4,0},{8,12},{12,8},{1,5},{5,1},{9,13},{13,9},{2,6},{6,2},{1... | collective-permute-start | bytes 958472 | tf_op jit(solution)/shard_map/ppermute | solution.py:48
  44.1 1.7 %collective-permute-start.16 = (bf16[208,768]{1,0:T(8,128)(2,1)S(1)}, bf16[208,768]{1,0:T(8,128)(2,1)S(1)}, u32[]{:S(2)}, u32[]{:S(2)}) collective-permute-start(bf16[208,768]{1,0:T(8,128)(2,1)S(1)} %collective-permute-done.15.refs_2_), channel_id=1, source_target_pairs={{0,4},{4,0},{8,12},{12,8},{1,5},{5,1},{9,13},{13,9},{2,6},{6,2},{1... | collective-permute-start | bytes 958472 | tf_op jit(solution)/shard_map/ppermute | solution.py:48

commit v3 on v2

--- a/solution.py
+++ b/solution.py
@@ -477,8 +477,8 @@
     row_at, col_at, img_at = lax.axis_index("row"), lax.axis_index("col"), lax.axis_index("img")
     row_bits = bits_of(row)
     far, rest = row_bits[0], row_bits[1:]
-    relays = img if triple_t.shape[0] % (16 * (img + 1)) == 0 else 0
-    piece_rows = triple_t.shape[0] // (relays + 1)
+    piece_rows = triple_t.shape[0] * 5 // (8 * img) // 16 * 16
+    relays = img if piece_rows else 0
     starts = [(img_at - k) % img for k in range(relays)] + [jnp.int32(relays)]
     place = [row_at == 0, row_at == row - 1, col_at == 0, col_at == col - 1, row_at % 2 == 0, col_at % 2 == 0, row_at]
     place = jnp.stack([jnp.asarray(p).astype(jnp.int32) for p in place + [start * piece_rows for start in starts]])
@@ -486,7 +486,7 @@
     mine, last = pl.pallas_call(
         piece_kernel,
         out_shape=(
-            pltpu.VMEM((piece_rows, channels), jnp.bfloat16),
+            pltpu.VMEM((max(piece_rows, 16), channels), jnp.bfloat16),
             pltpu.VMEM((triple_t.shape[0] - relays * piece_rows, channels), jnp.bfloat16),
         ),
         in_specs=[scalars, hbm],
@@ -535,7 +535,7 @@
     far_pieces = []
     if relays:
         first = swapped(mine, "row", far)
-    far_last = swapped(after(last, even_rows, odd_rows), "row", far)
+    far_last = swapped(after(last, even_rows, odd_rows, first), "row", far)
 
     even_corners, odd_corners = pl.pallas_call(
         corner_kernel,
@@ -545,7 +545,7 @@
         compiler_params=small,
         cost_estimate=pl.CostEstimate(flops=1_000_000, bytes_accessed=1_000_000, transcendentals=0),
         name="corners",
-    )(place, after(even_rows, xq), after(odd_rows, even_cols, odd_cols))
+    )(place, after(even_rows, xq, first), after(odd_rows, even_cols, odd_cols))
     even_corners, odd_corners = pair_swapped(even_corners, odd_corners, "col")
 
     carriers = pl.pallas_call(
@@ -567,7 +567,9 @@
         carriers = carriers if len(parts) == 1 else jnp.concatenate(parts, axis=0)
         got = swapped(carriers, "col", 2 * bit - 1)
         parts.append(got)
+
     if relays:
+        first = after(first, even_corners, odd_corners, got)
         others = [lax.ppermute(first, "img", [(i, (i + k) % img) for i in range(img)]) for k in range(1, relays)]
         far_pieces = [first] + others
     far_pieces.append(far_last)

time: 59.4 us -> 64.4 us (1.084)
  the two profiles are of different devices: /device:TPU:9 before, /device:TPU:0 now
where the time goes in v3:
time: 64.4 us; the launch traced here: 64.1 us
  Pallas kernels  29.9 us (46%)
  starting transfers between devices  23.2 us (36%)
  waiting for transfers between devices  9.39 us (15%)
  between operations  0.86 us (1%)
  local copies, waits for them, and re-layouts  0.79 us (1%)
    ppermute x10, starting transfers between devices, swapped(): return lax.ppermute(block, axis, [(i, i ^ bit) for i in range(count)])  11.7 us
    ppermute x6, starting transfers between devices, pair_swapped(): got.append(lax.ppermute(block, axis, pairs + [(b, a) for a, b in pairs]))  10 us
    ppermute x10, waiting for transfers between devices, swapped(): return lax.ppermute(block, axis, [(i, i ^ bit) for i in range(count)])  9.37 us
    pallas_call x1, Pallas kernels, local(): pl.pallas_call(functools.partial(project_kernel, offsets, numbered, tripl...  8.22 us
    pallas_call x1, Pallas kernels, local(): pl.pallas_call(functools.partial(attend_kernel, rows // TILE, cols // TIL...  6.97 us
    pallas_call x1, Pallas kernels, local(): pl.pallas_call(functools.partial(carrier_kernel, offsets), out_shape=(jax...  3.86 us
    pallas_call x1, Pallas kernels, local(): pl.pallas_call(out_kernel, out_shape=jax.ShapeDtypeStruct(grid_elements.s...  2.35 us
    pallas_call x1, Pallas kernels, local(): pl.pallas_call(edge_kernel, out_shape=(pltpu.VMEM((rows, cols, LANES), jn...  2.26 us
  transfers between devices with their start and end apart: 17, of which 3 were waited for; matrix products, arithmetic and copies ran while one was open for 0% of the time, Pallas kernels for 23%

profile of v3, /device:TPU:0, one launch (start us, length us, event | category | flops | bytes accessed | tf_op | source)
XLA Modules:
  0.0 64.1 jit_solution(13991693217718374884)
XLA Ops:
  0.7 0.1 stack.63.place_ref
  0.8 1.6 %pieces.1 = (bf16[176,768]{1,0:T(8,128)(2,1)S(1)}, bf16[224,768]{1,0:T(8,128)(2,1)S(1)}) custom-call(s32[10]{0:T(128)S(1)} %stack.63.place_ref, bf16[576,768]{1,0:T(8,128)(2,1)} %bitcast.11), custom_call_target="tpu_custom_call" | custom-call | flops 1000000 | bytes 1000000 | tf_op jit(solution)/shard_map/pieces/pallas_call | solution.py:486
  2.4 3.0 %collective-permute-start.4 = (bf16[176,768]{1,0:T(8,128)(2,1)S(1)}, bf16[176,768]{1,0:T(8,128)(2,1)S(1)}, u32[]{:S(2)}, u32[]{:S(2)}) collective-permute-start(bf16[176,768]{1,0:T(8,128)(2,1)S(1)} %get-tuple-element.33), channel_id=1, source_target_pairs={{0,8},{4,12},{8,0},{12,4},{1,9},{5,13},{9,1},{13,5},{2,10},{6,14},... | collective-permute-start | bytes 811016 | tf_op jit(solution)/shard_map/ppermute | solution.py:48
  5.4 0.7 %copy-done.2 = bf16[2,2,768]{2,1,0:T(2,128)(2,1)S(1)} copy-done((bf16[2,2,768]{2,1,0:T(2,128)(2,1)S(1)}, bf16[2,2,768]{2,1,0:T(2,128)(2,1)}, u32[]{:S(2)}) %copy-start.2) | copy-done | bytes 6168
  6.1 2.3 %edge_rows.1 = (bf16[32,32,128]{2,1,0:T(8,128)(2,1)S(1)}, bf16[4,32,768]{2,1,0:T(8,128)(2,1)S(1)}, bf16[4,32,768]{2,1,0:T(8,128)(2,1)S(1)}, bf16[17,8,768]{2,1,0...) custom-call(s32[10]{0:T(128)S(1)} %stack.63.place_ref, s32[32,32]{1,0:T(8,128)} %flags_hbm.1, ...), custom_call_target="tpu_custom_call" | custom-call | flops 1000000 | bytes 1000000 | tf_op jit(solution)/shard_map/edge_rows/pallas_call | solution.py:501
  8.4 1.6 %collective-permute-start = (bf16[17,8,768]{2,1,0:T(8,128)(2,1)S(1)}, bf16[17,8,768]{2,1,0:T(8,128)(2,1)S(1)}, u32[]{:S(2)}, u32[]{:S(2)}) collective-permute-start(bf16[17,8,768]{2,1,0:T(8,128)(2,1)S(1)} %get-tuple-element.36), channel_id=1, source_target_pairs={{0,1},{2,3},{1,0},{3,2},{4,5},{6,7},{5,4},{7,6},{8,9},{10,11},{9,8... | collective-permute-start | bytes 626696 | tf_op jit(solution)/shard_map/ppermute | solution.py:42
  10.0 0.7 %collective-permute-start.1 = (bf16[16,8,768]{2,1,0:T(8,128)(2,1)S(1)}, bf16[16,8,768]{2,1,0:T(8,128)(2,1)S(1)}, u32[]{:S(2)}, u32[]{:S(2)}) collective-permute-start(bf16[16,8,768]{2,1,0:T(8,128)(2,1)S(1)} %get-tuple-element.37), channel_id=1, source_target_pairs={{1,2},{2,1},{5,6},{6,5},{9,10},{10,9},{13,14},{14,13},{17,18},{18,... | collective-permute-start | bytes 589832 | tf_op jit(solution)/shard_map/ppermute | solution.py:42
  10.7 0.7 %collective-permute-start.3 = (bf16[4,32,768]{2,1,0:T(8,128)(2,1)S(1)}, bf16[4,32,768]{2,1,0:T(8,128)(2,1)S(1)}, u32[]{:S(2)}, u32[]{:S(2)}) collective-permute-start(bf16[4,32,768]{2,1,0:T(8,128)(2,1)S(1)} %get-tuple-element.39), channel_id=1, source_target_pairs={{4,8},{8,4},{5,9},{9,5},{6,10},{10,6},{7,11},{11,7},{20,24},{24,20... | collective-permute-start | bytes 589832 | tf_op jit(solution)/shard_map/ppermute | solution.py:42
  11.4 1.9 %collective-permute-start.2 = (bf16[4,32,768]{2,1,0:T(8,128)(2,1)S(1)}, bf16[4,32,768]{2,1,0:T(8,128)(2,1)S(1)}, u32[]{:S(2)}, u32[]{:S(2)}) collective-permute-start(bf16[4,32,768]{2,1,0:T(8,128)(2,1)S(1)} %get-tuple-element.38), channel_id=1, source_target_pairs={{0,4},{8,12},{4,0},{12,8},{1,5},{9,13},{5,1},{13,9},{2,6},{10,14},... | collective-permute-start | bytes 589832 | tf_op jit(solution)/shard_map/ppermute | solution.py:42
  13.3 1.8 %own_norm.1.xq_ref.refs_8_ = bf16[1024,768]{1,0:T(8,128)(2,1)S(1)} custom-call(bf16[32,32,768]{2,1,0:T(8,128)(2,1)S(1)} %get-tuple-element.35.x_ref), custom_call_target="tpu_custom_call" | custom-call | flops 1000000 | bytes 1000000 | tf_op jit(solution)/shard_map/own_norm/pallas_call | solution.py:523
  15.1 0.0 collective-permute-done.1.refs_3_
  15.2 0.6 corners.1
  15.8 0.0 copy-start.1
  15.8 4.5 %collective-permute-start.5 = (bf16[4,8,768]{2,1,0:T(8,128)(2,1)S(1)}, bf16[4,8,768]{2,1,0:T(8,128)(2,1)S(1)}, u32[]{:S(2)}, u32[]{:S(2)}) collective-permute-start(bf16[4,8,768]{2,1,0:T(8,128)(2,1)S(1)} %get-tuple-element.42), channel_id=1, source_target_pairs={{0,1},{2,3},{1,0},{3,2},{4,5},{6,7},{5,4},{7,6},{8,9},{10,11},{9,8... | collective-permute-start | bytes 147464 | tf_op jit(solution)/shard_map/ppermute | solution.py:42
  20.2 0.7 %collective-permute-start.6 = (bf16[4,8,768]{2,1,0:T(8,128)(2,1)S(1)}, bf16[4,8,768]{2,1,0:T(8,128)(2,1)S(1)}, u32[]{:S(2)}, u32[]{:S(2)}) collective-permute-start(bf16[4,8,768]{2,1,0:T(8,128)(2,1)S(1)} %get-tuple-element.43), channel_id=1, source_target_pairs={{1,2},{2,1},{5,6},{6,5},{9,10},{10,9},{13,14},{14,13},{17,18},{18,... | collective-permute-start | bytes 147464 | tf_op jit(solution)/shard_map/ppermute | solution.py:42
  21.0 2.6 %collective-permute-start.7 = (bf16[8,768]{1,0:T(8,128)(2,1)S(1)}, bf16[8,768]{1,0:T(8,128)(2,1)S(1)}, u32[]{:S(2)}, u32[]{:S(2)}) collective-permute-start(bf16[8,768]{1,0:T(8,128)(2,1)S(1)} %carrier_pair.1.refs_0_), channel_id=1, source_target_pairs={{0,3},{1,2},{2,1},{3,0},{4,7},{5,6},{6,5},{7,4},{8,11},{9,10},{10,... | collective-permute-start | bytes 36872 | tf_op jit(solution)/shard_map/ppermute | solution.py:48
  23.5 3.0 %collective-permute-done.7.refs_1_ = bf16[8,768]{1,0:T(8,128)(2,1)S(1)} collective-permute-done((bf16[8,768]{1,0:T(8,128)(2,1)S(1)}, bf16[8,768]{1,0:T(8,128)(2,1)S(1)}, u32[]{:S(2)}, u32[]{:S(2)}) %collective-permute-start.7) | collective-permute-done | bytes 12320 | tf_op jit(solution)/shard_map/ppermute | solution.py:48
  26.5 0.2 collective-permute-start.8
  26.7 3.0 %collective-permute-start.12 = (bf16[224,768]{1,0:T(8,128)(2,1)S(1)}, bf16[224,768]{1,0:T(8,128)(2,1)S(1)}, u32[]{:S(2)}, u32[]{:S(2)}) collective-permute-start(bf16[224,768]{1,0:T(8,128)(2,1)S(1)} %get-tuple-element.52), channel_id=1, source_target_pairs={{0,8},{4,12},{8,0},{12,4},{1,9},{5,13},{9,1},{13,5},{2,10},{6,14},... | collective-permute-start | bytes 1032200 | tf_op jit(solution)/shard_map/ppermute | solution.py:48
  29.7 1.5 %collective-permute-start.10 = (bf16[176,768]{1,0:T(8,128)(2,1)S(1)}, bf16[176,768]{1,0:T(8,128)(2,1)S(1)}, u32[]{:S(2)}, u32[]{:S(2)}) collective-permute-start(bf16[176,768]{1,0:T(8,128)(2,1)S(1)} %collective-permute-done.4.refs_2_), channel_id=1, source_target_pairs={{0,16},{16,0},{1,17},{17,1},{2,18},{18,2},{3,19},{19,3},{4,20},{20... | collective-permute-start | bytes 811016 | tf_op jit(solution)/shard_map/ppermute | solution.py:573
  31.2 2.1 %halo_norm.1 = (bf16[1600,768]{1,0:T(8,128)(2,1)S(1)}, f32[16,8,256]{2,1,0:T(8,128)S(1)}) custom-call(s32[10]{0:T(128)S(1)} %stack.63.place_ref, bf16[1024,768]{1,0:T(8,128)(2,1)S(1)} %own_norm.1.xq_ref.refs_8_, bf16[32,32,128]{2,1,0:T(8,128)(2,1)S(1)} %get-tuple-element.47.mark_ref, bf16[4,32,768]{2,1,0:T(8,128)(2,1)S(1)} %collective-permute-done.2.even_rows_ref.refs_0_, ...), custom_call_target="tpu_custom_call" | custom-call | flops 10000000 | bytes 6000000 | tf_op jit(solution)/shard_map/halo_norm/pallas_call | solution.py:594
  33.3 5.0 %collective-permute-done.12.refs_6_ = bf16[224,768]{1,0:T(8,128)(2,1)S(1)} collective-permute-done((bf16[224,768]{1,0:T(8,128)(2,1)S(1)}, bf16[224,768]{1,0:T(8,128)(2,1)S(1)}, u32[]{:S(2)}, u32[]{:S(2)}) %collective-permute-start.12) | collective-permute-done | bytes 344096 | tf_op jit(solution)/shard_map/ppermute | solution.py:48
  38.4 0.5 collective-permute-start.9
  38.9 0.0 collective-permute-start.11
  38.9 1.8 %collective-permute-start.15 = (bf16[208,768]{1,0:T(8,128)(2,1)S(1)}, bf16[208,768]{1,0:T(8,128)(2,1)S(1)}, u32[]{:S(2)}, u32[]{:S(2)}) collective-permute-start(bf16[208,768]{1,0:T(8,128)(2,1)S(1)} %final_pack.1.refs_0_), channel_id=1, source_target_pairs={{0,8},{4,12},{8,0},{12,4},{1,9},{5,13},{9,1},{13,5},{2,10},{6,14},... | collective-permute-start | bytes 958472 | tf_op jit(solution)/shard_map/ppermute | solution.py:48
  40.7 0.2 collective-permute-start.14
  41.0 8.2 %project.1 = (bf16[3,1024,256]{2,1,0:T(8,128)(2,1)S(1)}, bf16[3,1600,256]{2,1,0:T(8,128)(2,1)S(1)}, bf16[3,1600,256]{2,1,0:T(8,128)(2,1)S(1)}, bf16[2304,768]{1,0:T(8,128)(2,1)S(1)}) custom-call(s32[10]{0:T(128)S(1)} %stack.63.place_ref, bf16[576,768]{1,0:T(8,128)(2,1)S(1)} %bitcast.13, bf16[576,768]{1,0:T(8,128)(2,1)S(1)} %collective-permute-done.8.refs_1_, ...), custom_call_target="tpu_custom_call" | custom-call | flops 5000000000 | bytes 14000000 | tf_op jit(solution)/shard_map/project/pallas_call | solution.py:623
  49.2 0.3 collective-permute-start.16
  49.6 1.3 %collective-permute-done.16.refs_3_ = bf16[208,768]{1,0:T(8,128)(2,1)S(1)} collective-permute-done((bf16[208,768]{1,0:T(8,128)(2,1)S(1)}, bf16[208,768]{1,0:T(8,128)(2,1)S(1)}, u32[]{:S(2)}, u32[]{:S(2)}) %collective-permute-start.16) | collective-permute-done | bytes 319520 | tf_op jit(solution)/shard_map/ppermute | solution.py:48
  50.9 3.9 %carriers.1 = (bf16[2,2,768]{2,1,0:T(2,128)(2,1)}, bf16[768,768]{1,0:T(8,128)(2,1)S(1)}, bf16[12,256,256]{2,1,0:T(8,128)(2,1)S(1)}, f32[8,768]{1,0:T(8,128)S(1)}) custom-call(s32[10]{0:T(128)S(1)} %stack.63.place_ref, bf16[2304,768]{1,0:T(8,128)(2,1)S(1)} %get-tuple-element.58.wt, bf16[208,768]{1,0:T(8,128)(2,1)S(1)} %final_pack.1.refs_0_, ...), custom_call_target="tpu_custom_call" | custom-call | flops 500000000 | bytes 5000000 | tf_op jit(solution)/shard_map/carriers/pallas_call | solution.py:644
  54.8 7.0 %attend.1.mix_s = bf16[1024,768]{1,0:T(8,128)(2,1)S(1)} custom-call(bf16[3,1024,256]{2,1,0:T(8,128)(2,1)S(1)} %get-tuple-element.54.q_s, bf16[3,1600,256]{2,1,0:T(8,128)(2,1)S(1)} %get-tuple-element.55.k_s, bf16[3,1600,256]{2,1,0:T(8,128)(2,1)S(1)} %get-tuple-element.56.v_s, f32[16,8,256]{2,1,0:T(8,128)S(1)} %get-tuple-element.57.hide_ref, ...), custom_call_target="tpu_custom_call" | custom-call | flops 4000000000 | bytes 12000000 | tf_op jit(solution)/shard_map/attend/pallas_call | solution.py:664
  61.8 2.3 %out.1 = bf16[32,32,768]{2,1,0:T(8,128)(2,1)} custom-call(bf16[32,32,768]{2,1,0:T(8,128)(2,1)S(1)} %get-tuple-element.35.x_ref, bf16[1024,768]{1,0:T(8,128)(2,1)S(1)} %attend.1.mix_s, bf16[768,768]{1,0:T(8,128)(2,1)S(1)} %get-tuple-element.62.wo), custom_call_target="tpu_custom_call" | custom-call | flops 1200000000 | bytes 6000000 | tf_op jit(solution)/shard_map/out/pallas_call | solution.py:679
  (20 shorter events, 0.1 us)
Async XLA Ops:
  2.4 12.8 %collective-permute-start.4 = (bf16[176,768]{1,0:T(8,128)(2,1)S(1)}, bf16[176,768]{1,0:T(8,128)(2,1)S(1)}, u32[]{:S(2)}, u32[]{:S(2)}) collective-permute-start(bf16[176,768]{1,0:T(8,128)(2,1)S(1)} %get-tuple-element.33), channel_id=1, source_target_pairs={{0,8},{4,12},{8,0},{12,4},{1,9},{5,13},{9,1},{13,5},{2,10},{6,14},... | collective-permute-start | bytes 811016 | tf_op jit(solution)/shard_map/ppermute | solution.py:48
  5.4 0.7 %copy-start.2 = (bf16[2,2,768]{2,1,0:T(2,128)(2,1)S(1)}, bf16[2,2,768]{2,1,0:T(2,128)(2,1)}, u32[]{:S(2)}) copy-start(bf16[2,2,768]{2,1,0:T(2,128)(2,1)} %own_ref.1) | copy-start | bytes 18436
  8.4 6.8 %collective-permute-start = (bf16[17,8,768]{2,1,0:T(8,128)(2,1)S(1)}, bf16[17,8,768]{2,1,0:T(8,128)(2,1)S(1)}, u32[]{:S(2)}, u32[]{:S(2)}) collective-permute-start(bf16[17,8,768]{2,1,0:T(8,128)(2,1)S(1)} %get-tuple-element.36), channel_id=1, source_target_pairs={{0,1},{2,3},{1,0},{3,2},{4,5},{6,7},{5,4},{7,6},{8,9},{10,11},{9,8... | collective-permute-start | bytes 626696 | tf_op jit(solution)/shard_map/ppermute | solution.py:42
  10.0 5.1 %collective-permute-start.1 = (bf16[16,8,768]{2,1,0:T(8,128)(2,1)S(1)}, bf16[16,8,768]{2,1,0:T(8,128)(2,1)S(1)}, u32[]{:S(2)}, u32[]{:S(2)}) collective-permute-start(bf16[16,8,768]{2,1,0:T(8,128)(2,1)S(1)} %get-tuple-element.37), channel_id=1, source_target_pairs={{1,2},{2,1},{5,6},{6,5},{9,10},{10,9},{13,14},{14,13},{17,18},{18,... | collective-permute-start | bytes 589832 | tf_op jit(solution)/shard_map/ppermute | solution.py:42
  10.7 4.4 %collective-permute-start.3 = (bf16[4,32,768]{2,1,0:T(8,128)(2,1)S(1)}, bf16[4,32,768]{2,1,0:T(8,128)(2,1)S(1)}, u32[]{:S(2)}, u32[]{:S(2)}) collective-permute-start(bf16[4,32,768]{2,1,0:T(8,128)(2,1)S(1)} %get-tuple-element.39), channel_id=1, source_target_pairs={{4,8},{8,4},{5,9},{9,5},{6,10},{10,6},{7,11},{11,7},{20,24},{24,20... | collective-permute-start | bytes 589832 | tf_op jit(solution)/shard_map/ppermute | solution.py:42
  11.4 3.8 %collective-permute-start.2 = (bf16[4,32,768]{2,1,0:T(8,128)(2,1)S(1)}, bf16[4,32,768]{2,1,0:T(8,128)(2,1)S(1)}, u32[]{:S(2)}, u32[]{:S(2)}) collective-permute-start(bf16[4,32,768]{2,1,0:T(8,128)(2,1)S(1)} %get-tuple-element.38), channel_id=1, source_target_pairs={{0,4},{8,12},{4,0},{12,8},{1,5},{9,13},{5,1},{13,9},{2,6},{10,14},... | collective-permute-start | bytes 589832 | tf_op jit(solution)/shard_map/ppermute | solution.py:42
  13.3 13.2 %copy-start = (bf16[768,576]{0,1:T(8,128)(2,1)S(1)}, bf16[768,576]{0,1:T(8,128)(2,1)}, u32[]{:S(2)}) copy-start(bf16[768,576]{0,1:T(8,128)(2,1)} %param.7) | copy-start | bytes 2654212
  15.8 23.1 %copy-start.1 = (bf16[768,192]{0,1:T(8,128)(2,1)S(1)}, bf16[768,192]{0,1:T(8,128)(2,1)}, u32[]{:S(2)}) copy-start(bf16[768,192]{0,1:T(8,128)(2,1)} %param.8) | copy-start | bytes 884740
  15.8 10.7 %collective-permute-start.5 = (bf16[4,8,768]{2,1,0:T(8,128)(2,1)S(1)}, bf16[4,8,768]{2,1,0:T(8,128)(2,1)S(1)}, u32[]{:S(2)}, u32[]{:S(2)}) collective-permute-start(bf16[4,8,768]{2,1,0:T(8,128)(2,1)S(1)} %get-tuple-element.42), channel_id=1, source_target_pairs={{0,1},{2,3},{1,0},{3,2},{4,5},{6,7},{5,4},{7,6},{8,9},{10,11},{9,8... | collective-permute-start | bytes 147464 | tf_op jit(solution)/shard_map/ppermute | solution.py:42
  20.2 6.3 %collective-permute-start.6 = (bf16[4,8,768]{2,1,0:T(8,128)(2,1)S(1)}, bf16[4,8,768]{2,1,0:T(8,128)(2,1)S(1)}, u32[]{:S(2)}, u32[]{:S(2)}) collective-permute-start(bf16[4,8,768]{2,1,0:T(8,128)(2,1)S(1)} %get-tuple-element.43), channel_id=1, source_target_pairs={{1,2},{2,1},{5,6},{6,5},{9,10},{10,9},{13,14},{14,13},{17,18},{18,... | collective-permute-start | bytes 147464 | tf_op jit(solution)/shard_map/ppermute | solution.py:42
  21.0 5.6 %collective-permute-start.7 = (bf16[8,768]{1,0:T(8,128)(2,1)S(1)}, bf16[8,768]{1,0:T(8,128)(2,1)S(1)}, u32[]{:S(2)}, u32[]{:S(2)}) collective-permute-start(bf16[8,768]{1,0:T(8,128)(2,1)S(1)} %carrier_pair.1.refs_0_), channel_id=1, source_target_pairs={{0,3},{1,2},{2,1},{3,0},{4,7},{5,6},{6,5},{7,4},{8,11},{9,10},{10,... | collective-permute-start | bytes 36872 | tf_op jit(solution)/shard_map/ppermute | solution.py:48
  26.5 14.4 %collective-permute-start.8 = (bf16[576,768]{1,0:T(8,128)(2,1)S(1)}, bf16[576,768]{1,0:T(8,128)(2,1)S(1)}, u32[]{:S(2)}, u32[]{:S(2)}) collective-permute-start(bf16[576,768]{1,0:T(8,128)(2,1)S(1)} %bitcast.12), channel_id=1, source_target_pairs={{0,4},{4,0},{8,12},{12,8},{1,5},{5,1},{9,13},{13,9},{2,6},{6,2},{1... | collective-permute-start | bytes 2654216 | tf_op jit(solution)/shard_map/ppermute | solution.py:48
  26.7 11.6 %collective-permute-start.12 = (bf16[224,768]{1,0:T(8,128)(2,1)S(1)}, bf16[224,768]{1,0:T(8,128)(2,1)S(1)}, u32[]{:S(2)}, u32[]{:S(2)}) collective-permute-start(bf16[224,768]{1,0:T(8,128)(2,1)S(1)} %get-tuple-element.52), channel_id=1, source_target_pairs={{0,8},{4,12},{8,0},{12,4},{1,9},{5,13},{9,1},{13,5},{2,10},{6,14},... | collective-permute-start | bytes 1032200 | tf_op jit(solution)/shard_map/ppermute | solution.py:48
  29.7 9.2 %collective-permute-start.10 = (bf16[176,768]{1,0:T(8,128)(2,1)S(1)}, bf16[176,768]{1,0:T(8,128)(2,1)S(1)}, u32[]{:S(2)}, u32[]{:S(2)}) collective-permute-start(bf16[176,768]{1,0:T(8,128)(2,1)S(1)} %collective-permute-done.4.refs_2_), channel_id=1, source_target_pairs={{0,16},{16,0},{1,17},{17,1},{2,18},{18,2},{3,19},{19,3},{4,20},{20... | collective-permute-start | bytes 811016 | tf_op jit(solution)/shard_map/ppermute | solution.py:573
  38.4 2.6 %collective-permute-start.13 = (bf16[224,768]{1,0:T(8,128)(2,1)S(1)}, bf16[224,768]{1,0:T(8,128)(2,1)S(1)}, u32[]{:S(2)}, u32[]{:S(2)}) collective-permute-start(bf16[224,768]{1,0:T(8,128)(2,1)S(1)} %collective-permute-done.12.refs_6_), channel_id=1, source_target_pairs={{0,4},{4,0},{8,12},{12,8},{1,5},{5,1},{9,13},{13,9},{2,6},{6,2},{1... | collective-permute-start | bytes 1032200 | tf_op jit(solution)/shard_map/ppermute | solution.py:48
  38.4 2.4 %collective-permute-start.9 = (bf16[176,768]{1,0:T(8,128)(2,1)S(1)}, bf16[176,768]{1,0:T(8,128)(2,1)S(1)}, u32[]{:S(2)}, u32[]{:S(2)}) collective-permute-start(bf16[176,768]{1,0:T(8,128)(2,1)S(1)} %collective-permute-done.4.refs_2_), channel_id=1, source_target_pairs={{0,4},{4,0},{8,12},{12,8},{1,5},{5,1},{9,13},{13,9},{2,6},{6,2},{1... | collective-permute-start | bytes 811016 | tf_op jit(solution)/shard_map/ppermute | solution.py:48
  38.9 2.1 %collective-permute-start.11 = (bf16[176,768]{1,0:T(8,128)(2,1)S(1)}, bf16[176,768]{1,0:T(8,128)(2,1)S(1)}, u32[]{:S(2)}, u32[]{:S(2)}) collective-permute-start(bf16[176,768]{1,0:T(8,128)(2,1)S(1)} %collective-permute-done.10.refs_4_), channel_id=1, source_target_pairs={{0,4},{4,0},{8,12},{12,8},{1,5},{5,1},{9,13},{13,9},{2,6},{6,2},{1... | collective-permute-start | bytes 811016 | tf_op jit(solution)/shard_map/ppermute | solution.py:48
  38.9 10.3 %collective-permute-start.15 = (bf16[208,768]{1,0:T(8,128)(2,1)S(1)}, bf16[208,768]{1,0:T(8,128)(2,1)S(1)}, u32[]{:S(2)}, u32[]{:S(2)}) collective-permute-start(bf16[208,768]{1,0:T(8,128)(2,1)S(1)} %final_pack.1.refs_0_), channel_id=1, source_target_pairs={{0,8},{4,12},{8,0},{12,4},{1,9},{5,13},{9,1},{13,5},{2,10},{6,14},... | collective-permute-start | bytes 958472 | tf_op jit(solution)/shard_map/ppermute | solution.py:48
  40.7 8.8 %collective-permute-start.14 = (bf16[208,768]{1,0:T(8,128)(2,1)S(1)}, bf16[208,768]{1,0:T(8,128)(2,1)S(1)}, u32[]{:S(2)}, u32[]{:S(2)}) collective-permute-start(bf16[208,768]{1,0:T(8,128)(2,1)S(1)} %final_pack.1.refs_0_), channel_id=1, source_target_pairs={{0,4},{4,0},{8,12},{12,8},{1,5},{5,1},{9,13},{13,9},{2,6},{6,2},{1... | collective-permute-start | bytes 958472 | tf_op jit(solution)/shard_map/ppermute | solution.py:48
  49.2 1.7 %collective-permute-start.16 = (bf16[208,768]{1,0:T(8,128)(2,1)S(1)}, bf16[208,768]{1,0:T(8,128)(2,1)S(1)}, u32[]{:S(2)}, u32[]{:S(2)}) collective-permute-start(bf16[208,768]{1,0:T(8,128)(2,1)S(1)} %collective-permute-done.15.refs_2_), channel_id=1, source_target_pairs={{0,4},{4,0},{8,12},{12,8},{1,5},{5,1},{9,13},{13,9},{2,6},{6,2},{1... | collective-permute-start | bytes 958472 | tf_op jit(solution)/shard_map/ppermute | solution.py:48
